TPU v7x, 32 devices: a whole 2x2x4 slice. The times are simulated.
32 devices in a mesh: dp: 8 (over z, x), ctx: 4 (over y, core).
Axes of the slice: x: 2, y: 2, z: 4, core: 2. Of those that a mesh axis runs over, the one named last changes fastest.
Arguments:
- tokens: bfloat16 [64, 512, 960], P('dp', 'ctx'), may hold values from -6 to 6
- lengths: int32 [64], P('dp'), may hold values from 256 to 512, as said below
- gain_attn: bfloat16 [960], P('dp'), may hold values from 0.5 to 1.5
- w_query: bfloat16 [960, 960], P('dp', 'ctx'), may hold values from -0.1875 to 0.1875
- w_key: bfloat16 [960, 320], P('dp', 'ctx'), may hold values from -0.1875 to 0.1875
- w_value: bfloat16 [960, 320], P('dp', 'ctx'), may hold values from -0.1875 to 0.1875
- w_out: bfloat16 [960, 960], P('dp', 'ctx'), may hold values from -1.5 to 1.5
- gain_ffn: bfloat16 [960], P('dp'), may hold values from 0.5 to 1.5
- w_gate: bfloat16 [960, 2560], P('dp', 'ctx'), may hold values from -0.1875 to 0.1875
- w_up: bfloat16 [960, 2560], P('dp', 'ctx'), may hold values from -0.1875 to 0.1875
- w_down: bfloat16 [2560, 960], P('dp', 'ctx'), may hold values from -0.125 to 0.125
- grad_out: bfloat16 [64, 512, 960], P('dp', 'ctx'), may hold values from -6 to 6
Outputs:
- output: bfloat16 [64, 512, 960], P('dp', 'ctx')
- grad_tokens: bfloat16 [64, 512, 960], P('dp', 'ctx')
- grad_gain_attn: float32 [960], P('dp')
- grad_w_query: float32 [960, 960], P('dp', 'ctx')
- grad_w_key: float32 [960, 320], P('dp', 'ctx')
- grad_w_value: float32 [960, 320], P('dp', 'ctx')
- grad_w_out: float32 [960, 960], P('dp', 'ctx')
- grad_gain_ffn: float32 [960], P('dp')
- grad_w_gate: float32 [960, 2560], P('dp', 'ctx')
- grad_w_up: float32 [960, 2560], P('dp', 'ctx')
- grad_w_down: float32 [2560, 960], P('dp', 'ctx')
Inputs may be any that keep to these rules, and one draw needn't show every extreme that they name: `lengths`: in every aligned group of 8 sequences one is 512 long and one is 256 long.
All inputs are finite; a program needn't handle non-finite values.
Results may differ from a plain program's by a relative error of at most 0.015.
Values may be sent and summed in bfloat16 or wider, within the bound.
A program may use at most 192 MiB of HBM per device.

v0:
```python
from functools import partial

import jax
import jax.numpy as jnp
from jax import lax
from jax.sharding import PartitionSpec as P

HEADS = 15
KV_HEADS = 5
HEAD_DIM = 64
SEQ_MB = 4
BATCHES = 2


EPS = 1e-05
THETA = 100000.0


def product(former, latter):
    return jnp.dot(former, latter, preferred_element_type=jnp.float32)


def against(former, latter):
    return lax.dot_general(
        former, latter, (((1,), (1,)), ((), ())), preferred_element_type=jnp.float32
    )


def outer_sum(former, latter):
    return lax.dot_general(
        former, latter, (((0,), (0,)), ((), ())), preferred_element_type=jnp.float32
    )


def rms_scale(values, scaling):
    return values * lax.rsqrt(jnp.mean(values * values, axis=-1, keepdims=True) + EPS) * scaling


def rotate(values, cosine, sine_part):
    half_dim = values.shape[-1] // 2
    lower_half = values[..., :half_dim]
    upper_half = values[..., half_dim:]
    return jnp.concatenate(
        [
            lower_half * cosine - upper_half * sine_part,
            upper_half * cosine + lower_half * sine_part,
        ],
        axis=-1,
    )


def silu_gate(gating, up_proj):
    return gating * jax.nn.sigmoid(gating) * up_proj


def fetch(gain_attn, w_query, w_key, w_value, w_out, gain_ffn, w_gate, w_up, w_down):
    col_query, col_key, col_value, col_out, col_gate, col_up, col_down = (
        lax.all_gather(w_query, "ctx", axis=1, tiled=True),
        lax.all_gather(w_key, "ctx", axis=1, tiled=True),
        lax.all_gather(w_value, "ctx", axis=1, tiled=True),
        lax.all_gather(w_out, "ctx", axis=1, tiled=True),
        lax.all_gather(w_gate, "ctx", axis=1, tiled=True),
        lax.all_gather(w_up, "ctx", axis=1, tiled=True),
        lax.all_gather(w_down, "ctx", axis=1, tiled=True),
    )
    return (
        lax.all_gather(col_query, "dp", axis=0, tiled=True),
        lax.all_gather(col_key, "dp", axis=0, tiled=True),
        lax.all_gather(col_value, "dp", axis=0, tiled=True),
        lax.all_gather(col_out, "dp", axis=0, tiled=True),
        lax.all_gather(col_gate, "dp", axis=0, tiled=True),
        lax.all_gather(col_up, "dp", axis=0, tiled=True),
        lax.all_gather(col_down, "dp", axis=0, tiled=True),
        lax.all_gather(gain_attn, "dp", axis=0, tiled=True),
        lax.all_gather(gain_ffn, "dp", axis=0, tiled=True),
    )


def masked_scores(queries, key_block, allowed, factor):
    scores = (
        jnp.einsum("mcgd,mld->mgcl", queries, key_block, preferred_element_type=jnp.float32)
        * factor
    )
    return jnp.where(allowed, scores, -1e30)


def attend(operands, allowed, factor):
    queries, key_block, value_block = operands
    scores = masked_scores(queries, key_block, allowed, factor)
    peak = jnp.max(scores, axis=-1, keepdims=True)
    raised = jnp.exp(scores - peak)
    summed = jnp.sum(raised, axis=-1, keepdims=True)
    shares = (raised / summed).astype(jnp.bfloat16)
    blended = jnp.einsum("mgcl,mld->mcgd", shares, value_block, preferred_element_type=jnp.float32)
    return (blended.astype(jnp.bfloat16), peak + jnp.log(summed))


def attend_back(operands, allowed, factor):
    queries, key_block, value_block, upstream, logsum = operands
    scores = masked_scores(queries, key_block, allowed, factor)
    shares = jnp.exp(scores - logsum)
    d_values = jnp.einsum(
        "mgcl,mcgd->mld", shares.astype(jnp.bfloat16), upstream, preferred_element_type=jnp.float32
    )
    d_shares = jnp.einsum(
        "mcgd,mld->mgcl", upstream, value_block, preferred_element_type=jnp.float32
    )
    row_dot = jnp.sum(d_shares * shares, axis=-1, keepdims=True)
    d_scores = (shares * (d_shares - row_dot)).astype(jnp.bfloat16)
    d_queries = (
        jnp.einsum("mgcl,mld->mcgd", d_scores, key_block, preferred_element_type=jnp.float32)
        * factor
    )
    d_keys = (
        jnp.einsum("mgcl,mcgd->mld", d_scores, queries, preferred_element_type=jnp.float32) * factor
    )
    return (d_queries, d_keys, d_values)


def settle(
    grad_one, grad_query, grad_key, grad_value, grad_out, grad_two, grad_gate, grad_up, grad_down
):
    groups = lax.axis_size("ctx")
    wide_one = jnp.broadcast_to(grad_one[:, None], (grad_one.shape[0], groups))
    wide_two = jnp.broadcast_to(grad_two[:, None], (grad_two.shape[0], groups))
    sum_query, sum_key, sum_value, sum_out, sum_gate, sum_up, sum_down, sum_one, sum_two = (
        lax.psum_scatter(
            grad_query.astype(jnp.bfloat16), "ctx", scatter_dimension=1, tiled=True
        ).astype(jnp.float32),
        lax.psum_scatter(
            grad_key.astype(jnp.bfloat16), "ctx", scatter_dimension=1, tiled=True
        ).astype(jnp.float32),
        lax.psum_scatter(
            grad_value.astype(jnp.bfloat16), "ctx", scatter_dimension=1, tiled=True
        ).astype(jnp.float32),
        lax.psum_scatter(
            grad_out.astype(jnp.bfloat16), "ctx", scatter_dimension=1, tiled=True
        ).astype(jnp.float32),
        lax.psum_scatter(
            grad_gate.astype(jnp.bfloat16), "ctx", scatter_dimension=1, tiled=True
        ).astype(jnp.float32),
        lax.psum_scatter(
            grad_up.astype(jnp.bfloat16), "ctx", scatter_dimension=1, tiled=True
        ).astype(jnp.float32),
        lax.psum_scatter(
            grad_down.astype(jnp.bfloat16), "ctx", scatter_dimension=1, tiled=True
        ).astype(jnp.float32),
        lax.psum_scatter(
            wide_one.astype(jnp.bfloat16), "ctx", scatter_dimension=1, tiled=True
        ).astype(jnp.float32),
        lax.psum_scatter(
            wide_two.astype(jnp.bfloat16), "ctx", scatter_dimension=1, tiled=True
        ).astype(jnp.float32),
    )
    own_query, own_key, own_value, own_out, own_gate, own_up, own_down, own_one, own_two = (
        lax.psum_scatter(sum_query, "dp", scatter_dimension=0, tiled=True),
        lax.psum_scatter(sum_key, "dp", scatter_dimension=0, tiled=True),
        lax.psum_scatter(sum_value, "dp", scatter_dimension=0, tiled=True),
        lax.psum_scatter(sum_out, "dp", scatter_dimension=0, tiled=True),
        lax.psum_scatter(sum_gate, "dp", scatter_dimension=0, tiled=True),
        lax.psum_scatter(sum_up, "dp", scatter_dimension=0, tiled=True),
        lax.psum_scatter(sum_down, "dp", scatter_dimension=0, tiled=True),
        lax.psum_scatter(sum_one, "dp", scatter_dimension=0, tiled=True),
        lax.psum_scatter(sum_two, "dp", scatter_dimension=0, tiled=True),
    )
    return (
        own_one[:, 0],
        own_query,
        own_key,
        own_value,
        own_out,
        own_two[:, 0],
        own_gate,
        own_up,
        own_down,
    )


def on_device(
    tokens,
    lengths,
    gain_attn,
    w_query,
    w_key,
    w_value,
    w_out,
    gain_ffn,
    w_gate,
    w_up,
    w_down,
    grad_out,
):
    seq_count, span_len, width = tokens.shape
    groups = lax.axis_size("ctx")
    length = span_len * groups
    ctx_rank = lax.axis_index("ctx")
    batch_size = SEQ_MB
    per_kv = HEADS // KV_HEADS
    query_width = HEADS * HEAD_DIM
    key_width = KV_HEADS * HEAD_DIM
    factor = HEAD_DIM ** (-0.5)
    half_dim = HEAD_DIM // 2
    inverse = THETA ** (-(jnp.arange(half_dim, dtype=jnp.float32) * 2.0 / HEAD_DIM))
    query_pos = ctx_rank * span_len + jnp.arange(span_len, dtype=jnp.int32)
    angles = query_pos.astype(jnp.float32)[:, None] * inverse[None, :]
    cosine = jnp.cos(angles)
    sine_part = jnp.sin(angles)
    cos_query = cosine[:, None, None, :]
    sin_query = sine_part[:, None, None, :]
    cos_key = cosine[:, None, :]
    sin_key = sine_part[:, None, :]
    key_pos = jnp.arange(length, dtype=jnp.int32)
    causal = key_pos[None, :] <= query_pos[:, None]
    rows = batch_size * span_len
    shards = (gain_attn, w_query, w_key, w_value, w_out, gain_ffn, w_gate, w_up, w_down)
    results = []
    input_grads = []
    sums = None
    owned = None
    for micro in range(BATCHES):
        lower = micro * batch_size
        forward_weights = fetch(*shards)
        (
            full_query,
            full_key,
            full_value,
            full_out,
            full_gate,
            full_up,
            full_down,
            full_one,
            full_two,
        ) = forward_weights
        gain_one = full_one.astype(jnp.float32)
        gain_two = full_two.astype(jnp.float32)
        inputs = tokens[lower : lower + batch_size].astype(jnp.float32).reshape(rows, width)
        valid_len = lengths[lower : lower + batch_size]
        allowed = causal[None, None] & (
            key_pos[None, None, None, :] < valid_len[:, None, None, None]
        )
        normed_attn = rms_scale(inputs, gain_one).astype(jnp.bfloat16)
        queries = product(normed_attn, full_query).reshape(
            batch_size, span_len, KV_HEADS, per_kv, HEAD_DIM
        )
        queries = rotate(queries, cos_query, sin_query).astype(jnp.bfloat16)
        key_own = product(normed_attn, full_key).reshape(batch_size, span_len, KV_HEADS, HEAD_DIM)
        key_own = (
            rotate(key_own, cos_key, sin_key)
            .astype(jnp.bfloat16)
            .reshape(batch_size, span_len, key_width)
        )
        value_own = (
            product(normed_attn, full_value)
            .astype(jnp.bfloat16)
            .reshape(batch_size, span_len, key_width)
        )
        key_all, value_all = (
            lax.all_gather(key_own, "ctx", axis=1, tiled=True),
            lax.all_gather(value_own, "ctx", axis=1, tiled=True),
        )
        head_query = jnp.moveaxis(queries, 2, 0)
        head_key = jnp.moveaxis(key_all.reshape(batch_size, length, KV_HEADS, HEAD_DIM), 2, 0)
        head_value = jnp.moveaxis(value_all.reshape(batch_size, length, KV_HEADS, HEAD_DIM), 2, 0)
        blended, logsum = lax.map(
            partial(attend, allowed=allowed, factor=factor), (head_query, head_key, head_value)
        )
        attended = jnp.moveaxis(blended, 0, 2).reshape(rows, query_width)
        hidden = inputs + product(attended, full_out)
        normed_ffn = rms_scale(hidden, gain_two).astype(jnp.bfloat16)
        gating = product(normed_ffn, full_gate)
        up_proj = product(normed_ffn, full_up)
        inner = silu_gate(gating, up_proj).astype(jnp.bfloat16)
        result = hidden + product(inner, full_down)
        results.append(result.astype(jnp.bfloat16).reshape(batch_size, span_len, width))
        backward_weights = fetch(*shards)
        (
            back_query,
            back_key,
            back_value,
            back_out,
            back_gate,
            back_up,
            back_down,
            back_one,
            back_two,
        ) = backward_weights
        upstream = grad_out[lower : lower + batch_size].astype(jnp.float32).reshape(rows, width)
        d_down = upstream.astype(jnp.bfloat16)
        grad_down = outer_sum(inner, d_down)
        d_inner = against(d_down, back_down)
        gate_pull = jax.vjp(silu_gate, gating, up_proj)[1]
        d_gating, d_up = gate_pull(d_inner)
        d_gating = d_gating.astype(jnp.bfloat16)
        d_up = d_up.astype(jnp.bfloat16)
        grad_gate = outer_sum(normed_ffn, d_gating)
        grad_up = outer_sum(normed_ffn, d_up)
        d_normed_ffn = against(d_gating, back_gate) + against(d_up, back_up)
        ffn_pull = jax.vjp(rms_scale, hidden, back_two.astype(jnp.float32))[1]
        d_hidden_part, grad_two = ffn_pull(d_normed_ffn)
        d_hidden = upstream + d_hidden_part
        d_attn = d_hidden.astype(jnp.bfloat16)
        grad_out_w = outer_sum(attended, d_attn)
        d_attended = against(d_attn, back_out).astype(jnp.bfloat16)
        head_upstream = jnp.moveaxis(
            d_attended.reshape(batch_size, span_len, KV_HEADS, per_kv, HEAD_DIM), 2, 0
        )
        d_query_h, d_key_h, d_value_h = lax.map(
            partial(attend_back, allowed=allowed, factor=factor),
            (head_query, head_key, head_value, head_upstream, logsum),
        )
        d_key_full = jnp.moveaxis(d_key_h, 0, 2).reshape(batch_size, length, key_width)
        d_value_full = jnp.moveaxis(d_value_h, 0, 2).reshape(batch_size, length, key_width)
        d_key_own, d_value_own = (
            lax.psum_scatter(d_key_full, "ctx", scatter_dimension=1, tiled=True),
            lax.psum_scatter(d_value_full, "ctx", scatter_dimension=1, tiled=True),
        )
        d_query = (
            rotate(jnp.moveaxis(d_query_h, 0, 2), cos_query, -sin_query)
            .astype(jnp.bfloat16)
            .reshape(rows, query_width)
        )
        d_key = (
            rotate(d_key_own.reshape(batch_size, span_len, KV_HEADS, HEAD_DIM), cos_key, -sin_key)
            .astype(jnp.bfloat16)
            .reshape(rows, key_width)
        )
        d_value = d_value_own.astype(jnp.bfloat16).reshape(rows, key_width)
        grad_query = outer_sum(normed_attn, d_query)
        grad_key = outer_sum(normed_attn, d_key)
        grad_value = outer_sum(normed_attn, d_value)
        d_normed_attn = (
            against(d_query, back_query) + against(d_key, back_key) + against(d_value, back_value)
        )
        attn_pull = jax.vjp(rms_scale, inputs, back_one.astype(jnp.float32))[1]
        d_input_part, grad_one = attn_pull(d_normed_attn)
        input_grads.append(
            (d_hidden + d_input_part).astype(jnp.bfloat16).reshape(batch_size, span_len, width)
        )
        local_grads = (
            grad_one,
            grad_query,
            grad_key,
            grad_value,
            grad_out_w,
            grad_two,
            grad_gate,
            grad_up,
            grad_down,
        )
        sums = (
            local_grads
            if sums is None
            else tuple((before + after for before, after in zip(sums, local_grads)))
        )
    owned = settle(*sums)
    output_all = jnp.concatenate(results, axis=0)
    grads_all = jnp.concatenate(input_grads, axis=0)
    return (
        output_all,
        grads_all,
        owned[0],
        owned[1],
        owned[2],
        owned[3],
        owned[4],
        owned[5],
        owned[6],
        owned[7],
        owned[8],
    )


def solution(mesh):
    return jax.shard_map(
        on_device,
        mesh=mesh,
        in_specs=(
            P("dp", "ctx", None),
            P("dp"),
            P("dp"),
            P("dp", "ctx"),
            P("dp", "ctx"),
            P("dp", "ctx"),
            P("dp", "ctx"),
            P("dp"),
            P("dp", "ctx"),
            P("dp", "ctx"),
            P("dp", "ctx"),
            P("dp", "ctx", None),
        ),
        out_specs=(
            P("dp", "ctx", None),
            P("dp", "ctx", None),
            P("dp"),
            P("dp", "ctx"),
            P("dp", "ctx"),
            P("dp", "ctx"),
            P("dp", "ctx"),
            P("dp"),
            P("dp", "ctx"),
            P("dp", "ctx"),
            P("dp", "ctx"),
        ),
        check_vma=False,
    )
```

profile of v0, /device:TPU:0, one launch (start us, length us, event | category | flops | bytes accessed | tf_op | source)
XLA Modules:
  0.0 1455.2 jit_solution(4534328517841795769)
XLA Ops:
  18.1 32.8 %all-gather = bf16[8,120,320]{1,2,0:T(8,128)(2,1)S(1)} all-gather(bf16[1,120,320]{1,2,0:T(8,128)(2,1)S(1)} %bitcast.760), channel_id=1, replica_groups=mesh['dp'=8,'ctx'=4] {'dp'}, dimensions={0}, use_global_device_ids=true | all-gather | bytes 691200 | tf_op jit(solution)/shard_map/all_gather | solution.py:69
  53.7 21.2 %all-reduce.11 = (bf16[960]{0:T(1024)(128)(2,1)S(1)}, bf16[960]{0:T(1024)(128)(2,1)S(1)}) all-reduce(bf16[960]{0:T(1024)(128)(2,1)S(1)} %dynamic-update-slice, bf16[960]{0:T(1024)(128)(2,1)S(1)} %dynamic-update-slice.1), channel_id=1, replica_groups=mesh['dp'=8,'ctx'=4] {'dp'}, use_global_device_ids=true, to_apply=%add | all-reduce | flops 1920 | bytes 7680
  83.3 31.6 %all-gather.1 = bf16[8,120,320]{1,2,0:T(8,128)(2,1)S(1)} all-gather(bf16[1,120,320]{1,2,0:T(8,128)(2,1)S(1)} %bitcast.761), channel_id=1, replica_groups=mesh['dp'=8,'ctx'=4] {'dp'}, dimensions={0}, use_global_device_ids=true | all-gather | bytes 691200 | tf_op jit(solution)/shard_map/all_gather | solution.py:68
  139.9 8.3 all_gather.52
  148.2 11.9 all_gather.54
  160.2 8.0 all-gather.2
  183.0 47.6 %all-gather.17.cloned.1.call-done = bf16[960,960]{1,0:T(8,128)(2,1)} async-done(((bf16[120,960]{1,0:T(8,128)(2,1)}), bf16[960,960]{1,0:T(8,128)(2,1)}) %all-gather.17.cloned.1.call-update) | async-done | bytes 1843216 | tf_op jit(solution)/shard_map/all_gather | solution.py:67
  241.4 21.8 %while.57 = (s32[]{:T(128)}, bf16[5,4,128,3,64]{2,4,3,1,0:T(8,128)(2,1)}, f32[5,4,3,128,1]{3,2,1,4,0:T(4,128)S(1)}, bf16[5,4,512,64]{2,3,1,0:T(8,128)(2,1)}, bf1...) while((s32[]{:T(128)}, ...), condition=%wide.region_10.11_spmd.clone, body=%wide.region_7.10_spmd.clone.sunk | while | flops 211122688 | bytes 11528297 | solution.py:264
  269.5 26.6 %while.56 = (s32[]{:T(128)}, bf16[5,4,128,3,64]{2,4,3,1,0:T(8,128)(2,1)}, f32[5,4,3,128,1]{3,2,1,4,0:T(4,128)S(1)}, bf16[5,4,512,64]{2,3,1,0:T(8,128)(2,1)}, bf1...) while((s32[]{:T(128)}, ...), condition=%wide.region_4.5_spmd.clone, body=%wide.region_1.4_spmd.clone.sunk | while | flops 211122688 | bytes 11528297 | solution.py:264
  305.4 58.1 %all-gather.21.cloned.1.call-done = bf16[960,2560]{1,0:T(8,128)(2,1)} async-done(((bf16[120,2560]{1,0:T(8,128)(2,1)}), bf16[960,2560]{1,0:T(8,128)(2,1)}) %all-gather.21.cloned.1.call-update) | async-done | bytes 4915216 | tf_op jit(solution)/shard_map/all_gather | solution.py:71
  370.5 75.7 %all-gather.23.cloned.1.call-done = bf16[960,2560]{1,0:T(8,128)(2,1)} async-done(((bf16[120,2560]{1,0:T(8,128)(2,1)}), bf16[960,2560]{1,0:T(8,128)(2,1)}) %all-gather.23.cloned.1.call-update) | async-done | bytes 4915216 | tf_op jit(solution)/shard_map/all_gather | solution.py:72
  453.1 79.7 %all-gather.25.cloned.1.call-done = bf16[2560,960]{1,0:T(8,128)(2,1)} async-done(((bf16[320,960]{1,0:T(8,128)(2,1)}), bf16[2560,960]{1,0:T(8,128)(2,1)}) %all-gather.25.cloned.1.call-update) | async-done | bytes 4915216 | tf_op jit(solution)/shard_map/all_gather | solution.py:73
  532.8 10.5 multiply_convert_fusion.1
  564.9 46.1 %while.58 = (s32[]{:T(128)}, f32[5,4,128,3,64]{2,4,3,0,1:T(8,128)}, f32[5,4,512,64]{2,3,0,1:T(8,128)}, f32[5,4,512,64]{2,3,0,1:T(8,128)}, bf16[5,4,512,64]{2,3,1...) while((s32[]{:T(128)}, f32[5,4,128,3,64]{2,4,3,0,1:T(8,128)}, ...), condition=%wide.region_15.16_spmd.clone, body=%wide.region_13.15_spmd.clone.sunk | while | flops 510884352 | bytes 27237504 | solution.py:307
  623.1 10.9 multiply_convert_fusion
  650.9 55.9 %while.59 = (s32[]{:T(128)}, f32[5,4,128,3,64]{2,4,3,0,1:T(8,128)}, f32[5,4,512,64]{2,3,0,1:T(8,128)S(1)}, f32[5,4,512,64]{2,3,0,1:T(8,128)}, bf16[5,4,512,64]{2...) while((s32[]{:T(128)}, f32[5,4,128,3,64]{2,4,3,0,1:T(8,128)}, ...), condition=%wide.region_22.23_spmd.clone, body=%wide.region_20.22_spmd.clone.sunk | while | flops 510884352 | bytes 27235456 | solution.py:307
  744.5 8.0 copy.249
  761.9 7.9 copy.251
  787.5 28.2 %reduce-scatter.37.cloned.1.call-done = f32[4,128,320]{1,2,0:T(8,128)} async-done(((f32[4,512,320]{1,2,0:T(8,128)}), f32[4,128,320]{1,2,0:T(8,128)}) %reduce-scatter.37.cloned.1.call-update) | async-done | bytes 655376 | tf_op jit(solution)/shard_map/reduce_scatter | solution.py:315
  818.7 30.0 %reduce-scatter.53.cloned.1.call-done = bf16[240,960]{1,0:T(8,128)(2,1)} async-done(((bf16[960,960]{1,0:T(8,128)(2,1)}), bf16[240,960]{1,0:T(8,128)(2,1)}) %reduce-scatter.53.cloned.1.call-update) | async-done | bytes 460816
  851.2 30.9 %reduce-scatter.55.cloned.1.call-done = bf16[240,960]{1,0:T(8,128)(2,1)} async-done(((bf16[960,960]{1,0:T(8,128)(2,1)}), bf16[240,960]{1,0:T(8,128)(2,1)}) %reduce-scatter.55.cloned.1.call-update) | async-done | bytes 460816
  884.4 51.4 %reduce-scatter.57.cloned.1.call-done = bf16[640,960]{1,0:T(8,128)(2,1)} async-done(((bf16[2560,960]{1,0:T(8,128)(2,1)}), bf16[640,960]{1,0:T(8,128)(2,1)}) %reduce-scatter.57.cloned.1.call-update) | async-done | bytes 1228816
  939.7 50.1 %reduce-scatter.59.cloned.1.call-done = bf16[640,960]{1,0:T(8,128)(2,1)} async-done(((bf16[2560,960]{1,0:T(8,128)(2,1)}), bf16[640,960]{1,0:T(8,128)(2,1)}) %reduce-scatter.59.cloned.1.call-update) | async-done | bytes 1228816
  1003.2 38.3 %reduce-scatter.51.cloned.1.call-done = bf16[2560,240]{0,1:T(8,128)(2,1)} async-done(((bf16[2560,960]{0,1:T(8,128)(2,1)}), bf16[2560,240]{0,1:T(8,128)(2,1)}) %reduce-scatter.51.cloned.1.call-update) | async-done | bytes 1228816 | tf_op jit(solution)/shard_map/reduce_scatter | solution.py:145
  1065.6 10.2 all-reduce.12
  1078.5 13.2 reduce-scatter.47.cloned.1.call-done
  1091.7 47.3 %all-reduce.14 = (f32[960,1]{0,1:T(1,128)S(1)}, f32[960,80]{0,1:T(8,128)S(1)}, f32[960,80]{0,1:T(8,128)S(1)}, f32[960,1]{0,1:T(1,128)S(1)}) all-reduce(f32[960,1]{0,1:T(1,128)S(1)} %dynamic-slice_convert_fusion.1, bf16[960,80]{0,1:T(8,128)(2,1)} %reduce-scatter.45.cloned.1.call-done, ...), channel_id=7, replica_groups=mesh['dp'=8,'ctx'=4] {'dp'}, use_global_device_ids=true, to_apply=%region_29.30.clone | all-reduce | flops 155520 | bytes 936960
  1141.6 19.6 %reduce-scatter.43.cloned.1.call-done = f32[120,240]{1,0:T(8,128)} async-done(((f32[960,240]{1,0:T(8,128)}), f32[120,240]{1,0:T(8,128)}) %reduce-scatter.43.cloned.1.call-update) | async-done | bytes 115216 | tf_op jit(solution)/shard_map/reduce_scatter | solution.py:156
  1161.2 66.3 %reduce-scatter.49.cloned.1.call-done = f32[120,240]{1,0:T(8,128)} async-done(((f32[960,240]{1,0:T(8,128)}), f32[120,240]{1,0:T(8,128)}) %reduce-scatter.49.cloned.1.call-update) | async-done | bytes 115216 | tf_op jit(solution)/shard_map/reduce_scatter | solution.py:159
  1227.5 73.7 %reduce-scatter.63.cloned.1.call-done = f32[120,640]{1,0:T(8,128)} async-done(((f32[960,640]{1,0:T(8,128)}), f32[120,640]{1,0:T(8,128)}) %reduce-scatter.63.cloned.1.call-update) | async-done | bytes 307216
  1301.2 73.4 %reduce-scatter.65.cloned.1.call-done = f32[120,640]{1,0:T(8,128)} async-done(((f32[960,640]{1,0:T(8,128)}), f32[120,640]{1,0:T(8,128)}) %reduce-scatter.65.cloned.1.call-update) | async-done | bytes 307216
  1374.6 73.9 %reduce-scatter.61.cloned.1.call-done = f32[320,240]{1,0:T(8,128)} async-done(((f32[2560,240]{1,0:T(8,128)}), f32[320,240]{1,0:T(8,128)}) %reduce-scatter.61.cloned.1.call-update) | async-done | bytes 307216
  (545 shorter events, 418.5 us)
Async XLA Ops:
  7.2 166.7 %all-gather.27.cloned.1.call-start = ((), (), s32[]{:S(2)}) async-start(), calls=%async_computation.23 | async-start | bytes 1638400 | tf_op jit(solution)/shard_map/all_gather | solution.py:259
  11.5 106.4 %copy-start.69 = (f32[4,128]{1,0:T(4,128)}, f32[4,128]{1,0:T(4,128)S(1)}, u32[]{:S(2)}) copy-start(f32[4,128]{1,0:T(4,128)S(1)} %get-tuple-element.501) | copy-start | bytes 6148
  74.9 162.5 %copy-start.63 = (f32[960]{0:T(1024)}, f32[960]{0:T(1024)S(1)}, u32[]{:S(2)}) copy-start(f32[960]{0:T(1024)S(1)} %convert_element_type.268) | copy-start | bytes 11524
  77.9 98.5 %all-gather.29.cloned.1.call-start = ((), (), s32[]{:S(2)}) async-start(), calls=%async_computation.24 | async-start | bytes 1638400 | tf_op jit(solution)/shard_map/all_gather | solution.py:258
  117.9 116.6 %copy-start.73 = (f32[4,128]{1,0:T(4,128)}, f32[4,128]{1,0:T(4,128)S(1)}, u32[]{:S(2)}) copy-start(f32[4,128]{1,0:T(4,128)S(1)} %get-tuple-element.653) | copy-start | bytes 6148
  117.9 119.5 %copy-start.79 = (f32[4,128]{1,0:T(4,128)}, f32[4,128]{1,0:T(4,128)S(1)}, u32[]{:S(2)}) copy-start(f32[4,128]{1,0:T(4,128)S(1)} %get-tuple-element.654) | copy-start | bytes 6148
  118.7 120.0 %copy-start.54 = (f32[128,32]{0,1:T(8,128)}, f32[128,32]{0,1:T(8,128)S(1)}, u32[]{:S(2)}) copy-start(f32[128,32]{0,1:T(8,128)S(1)} %get-tuple-element.639) | copy-start | bytes 49156
  120.9 57.0 %all-gather.13.cloned.1.call-start = ((), (), s32[]{:S(2)}) async-start(), calls=%async_computation.16 | async-start | bytes 1638400 | tf_op jit(solution)/shard_map/all_gather | solution.py:259
  124.0 56.5 %all-gather.15.cloned.1.call-start = ((), (), s32[]{:S(2)}) async-start(), calls=%async_computation.17 | async-start | bytes 1638400 | tf_op jit(solution)/shard_map/all_gather | solution.py:258
  124.8 105.8 %all-gather.17.cloned.1.call-start = ((), (), s32[]{:S(2)}) async-start(), calls=%async_computation.18 | async-start | bytes 2211840 | tf_op jit(solution)/shard_map/all_gather | solution.py:67
  133.0 166.2 %all-gather.19.cloned.1.call-start = ((), (), s32[]{:S(2)}) async-start(), calls=%async_computation.19 | async-start | bytes 2211840 | tf_op jit(solution)/shard_map/all_gather | solution.py:70
  139.8 223.7 %all-gather.21.cloned.1.call-start = ((), (), s32[]{:S(2)}) async-start(), calls=%async_computation.20 | async-start | bytes 5529600 | tf_op jit(solution)/shard_map/all_gather | solution.py:71
  148.2 298.0 %all-gather.23.cloned.1.call-start = ((), (), s32[]{:S(2)}) async-start(), calls=%async_computation.21 | async-start | bytes 5529600 | tf_op jit(solution)/shard_map/all_gather | solution.py:72
  160.2 372.7 %all-gather.25.cloned.1.call-start = ((), (), s32[]{:S(2)}) async-start(), calls=%async_computation.22 | async-start | bytes 5898240 | tf_op jit(solution)/shard_map/all_gather | solution.py:73
  170.2 610.0 %reduce-scatter.35.cloned.1.call-start = ((), (), s32[]{:S(2)}) async-start(), calls=%async_computation.25 | async-start | bytes 3276800 | tf_op jit(solution)/shard_map/reduce_scatter | solution.py:314
  305.4 140.8 %copy-start.16 = (bf16[512,960]{0,1:T(8,128)(2,1)}, bf16[512,960]{0,1:T(8,128)(2,1)S(1)}, u32[]{:S(2)}) copy-start(bf16[512,960]{0,1:T(8,128)(2,1)S(1)} %multiply_convert_fusion.6) | copy-start | bytes 2949124
  370.5 162.4 %copy-start.42 = (bf16[4,120,8,128]{3,2,1,0:T(8,128)(2,1)S(1)}, bf16[4,120,8,128]{3,2,1,0:T(8,128)(2,1)}, u32[]{:S(2)}) copy-start(bf16[4,120,8,128]{3,2,1,0:T(8,128)(2,1)} %get-tuple-element.611) | copy-start | bytes 2949124
  647.1 133.0 %reduce-scatter.39.cloned.1.call-start = ((), (), s32[]{:S(2)}) async-start(), calls=%async_computation.27 | async-start | bytes 3276800 | tf_op jit(solution)/shard_map/reduce_scatter | solution.py:314
  708.3 76.4 %reduce-scatter.41.cloned.1.call-start = ((), (), s32[]{:S(2)}) async-start(), calls=%async_computation.28 | async-start | bytes 3276800 | tf_op jit(solution)/shard_map/reduce_scatter | solution.py:315
  708.9 106.8 %reduce-scatter.37.cloned.1.call-start = ((), (), s32[]{:S(2)}) async-start(), calls=%async_computation.26 | async-start | bytes 3276800 | tf_op jit(solution)/shard_map/reduce_scatter | solution.py:315
  709.6 139.1 %reduce-scatter.53.cloned.1.call-start = ((), (), s32[]{:S(2)}) async-start(), calls=%async_computation.34 | async-start | bytes 2457600
  723.5 158.6 %reduce-scatter.55.cloned.1.call-start = ((), (), s32[]{:S(2)}) async-start(), calls=%async_computation.35 | async-start | bytes 2457600
  734.2 201.6 %reduce-scatter.57.cloned.1.call-start = ((), (), s32[]{:S(2)}) async-start(), calls=%async_computation.36 | async-start | bytes 6553600
  752.5 237.3 %reduce-scatter.59.cloned.1.call-start = ((), (), s32[]{:S(2)}) async-start(), calls=%async_computation.37 | async-start | bytes 6553600
  769.8 271.7 %reduce-scatter.51.cloned.1.call-start = ((), (), s32[]{:S(2)}) async-start(), calls=%async_computation.33 | async-start | bytes 6144000 | tf_op jit(solution)/shard_map/reduce_scatter | solution.py:145
  780.0 298.5 %reduce-scatter.45.cloned.1.call-start = ((), (), s32[]{:S(2)}) async-start(), calls=%async_computation.30 | async-start | bytes 819200 | tf_op jit(solution)/shard_map/reduce_scatter | solution.py:130
  784.6 307.1 %reduce-scatter.47.cloned.1.call-start = ((), (), s32[]{:S(2)}) async-start(), calls=%async_computation.31 | async-start | bytes 819200 | tf_op jit(solution)/shard_map/reduce_scatter | solution.py:133
  818.7 342.5 %reduce-scatter.43.cloned.1.call-start = ((), (), s32[]{:S(2)}) async-start(), calls=%async_computation.29 | async-start | bytes 1105920 | tf_op jit(solution)/shard_map/reduce_scatter | solution.py:156
  851.1 376.4 %reduce-scatter.49.cloned.1.call-start = ((), (), s32[]{:S(2)}) async-start(), calls=%async_computation.32 | async-start | bytes 1105920 | tf_op jit(solution)/shard_map/reduce_scatter | solution.py:159
  884.4 416.9 %reduce-scatter.63.cloned.1.call-start = ((), (), s32[]{:S(2)}) async-start(), calls=%async_computation.39 | async-start | bytes 2764800
  939.6 435.0 %reduce-scatter.65.cloned.1.call-start = ((), (), s32[]{:S(2)}) async-start(), calls=%async_computation.40 | async-start | bytes 2764800
  993.5 455.0 %reduce-scatter.61.cloned.1.call-start = ((), (), s32[]{:S(2)}) async-start(), calls=%async_computation.38 | async-start | bytes 2949120
  (93 other events, 785.8 us)
Sparse Core Ops, SparseCore 0:
  78.0 15.6 all-gather.26
  121.0 16.9 all-gather.28
  139.6 21.6 all-gather.12
  162.6 17.8 all-gather.14
  183.1 47.4 all-gather.16
  233.3 46.5 all-gather.18
  282.1 81.3 all-gather.20
  365.7 80.4 all-gather.22
  448.3 84.4 all-gather.24
  647.3 32.8 reduce-scatter.34
  708.4 32.7 reduce-scatter.38
  743.6 34.6 reduce-scatter.40
  781.0 34.6 reduce-scatter.36
  818.1 30.6 reduce-scatter.52
  851.4 30.6 reduce-scatter.54
  884.4 51.3 reduce-scatter.56
  938.4 51.3 reduce-scatter.58
  992.2 49.1 reduce-scatter.50
  1044.2 22.4 reduce-scatter.44
  1069.2 22.4 reduce-scatter.46
  1096.0 65.1 reduce-scatter.42
  1165.1 62.3 reduce-scatter.48
  1232.2 69.0 reduce-scatter.62
  1305.7 68.8 reduce-scatter.64
  1379.1 69.3 reduce-scatter.60
where the time goes:
time: 1470 us; the launch traced here: 1460 us
  waiting for transfers between devices  812 us (55%)
  matrix products  276 us (19%)
  blocking collectives  196 us (13%)
  local copies, waits for them, and re-layouts  110 us (7%)
  other arithmetic  41.2 us (3%)
  between operations  17.2 us (1%)
    unnamed x32, waiting for transfers between devices  385 us
    all_gather x1, waiting for transfers between devices, fetch(): lax.all_gather(col_down, 'dp', axis=0, tiled=True)  79.7 us
    unnamed x3, blocking collectives  78.7 us
    all_gather x1, waiting for transfers between devices, fetch(): lax.all_gather(col_up, 'dp', axis=0, tiled=True)  75.7 us
    unnamed x229, local copies, waits for them, and re-layouts  70.8 us
    reduce_scatter x1, waiting for transfers between devices, settle(): lax.psum_scatter(sum_out, 'dp', scatter_dimension=0, tiled=True)  66.3 us
    all_gather x1, waiting for transfers between devices, fetch(): lax.all_gather(col_gate, 'dp', axis=0, tiled=True)  58.1 us
    dot_general x14, matrix products, product(): return jnp.dot(former, latter, preferred_element_type=jnp.float32)  55.3 us
  transfers between devices with their start and end apart: 25, of which 17 were waited for; matrix products, arithmetic and copies ran while one was open for 20% of the time, Pallas kernels for 0%

commit v1 on v0

v1 whole, which is shorter than its diff:
```python
from functools import partial

import jax
import jax.numpy as jnp
from jax import lax
from jax.experimental import pallas as pl
from jax.experimental.pallas import tpu as pltpu
from jax.sharding import PartitionSpec as P

HEADS = 15
KV_HEADS = 5
HEAD_DIM = 64
PAIR = 2
PIECES = 4
MESH = pl.DeviceIdType.MESH

EPS = 1e-05
THETA = 100000.0


def product(former, latter):
    return jnp.dot(former, latter, preferred_element_type=jnp.float32)


def against(former, latter):
    return lax.dot_general(
        former, latter, (((1,), (1,)), ((), ())), preferred_element_type=jnp.float32
    )


def outer_sum(former, latter):
    return lax.dot_general(
        former, latter, (((0,), (0,)), ((), ())), preferred_element_type=jnp.float32
    )


def rms_scale(values, scaling):
    return values * lax.rsqrt(jnp.mean(values * values, axis=-1, keepdims=True) + EPS) * scaling


def rotate(values, cosine, sine_part):
    half_dim = values.shape[-1] // 2
    lower_half = values[..., :half_dim]
    upper_half = values[..., half_dim:]
    return jnp.concatenate(
        [
            lower_half * cosine - upper_half * sine_part,
            upper_half * cosine + lower_half * sine_part,
        ],
        axis=-1,
    )


def silu_gate(gating, up_proj):
    return gating * jax.nn.sigmoid(gating) * up_proj


def place():
    dp, ctx = lax.axis_index("dp"), lax.axis_index("ctx")
    return dp // PAIR, dp % PAIR, ctx // PAIR, ctx % PAIR


def device(z, x, y, c):
    return (z * PAIR + x, y * PAIR + c)


def remote(source, target, send_sem, recv_sem, where):
    return pltpu.make_async_remote_copy(
        src_ref=source,
        dst_ref=target,
        send_sem=send_sem,
        recv_sem=recv_sem,
        device_id=where,
        device_id_type=MESH,
    )


def greet(z, x, y, c, depth):
    barrier = pltpu.get_barrier_semaphore()
    for where in (device(z, 1 - x, y, c), device(z, x, 1 - y, c), device(z, x, y, 1 - c)):
        pl.semaphore_signal(barrier, inc=1, device_id=where, device_id_type=MESH)

    @pl.when(z > 0)
    def _():
        pl.semaphore_signal(barrier, inc=1, device_id=device(z - 1, x, y, c), device_id_type=MESH)

    @pl.when(z < depth - 1)
    def _():
        pl.semaphore_signal(barrier, inc=1, device_id=device(z + 1, x, y, c), device_id_type=MESH)

    pl.semaphore_wait(barrier, 3 + jnp.minimum(z, 1) + jnp.minimum(depth - 1 - z, 1))


def gather_kernel(*refs):
    shards, fulls = refs[:PIECES], refs[PIECES : 2 * PIECES]
    local, z_send, z_recv, f_send, f_recv, s_send, s_recv, c_send, c_recv = refs[2 * PIECES :]
    depth = fulls[0].shape[2]
    z, x, y, c = place()
    greet(z, x, y, c, depth)

    def along_z(p, way, owner):
        shard = fulls[p].at[y, c, owner, x]
        return remote(
            shard,
            shard,
            z_send.at[way, p, owner],
            z_recv.at[way, p, owner],
            device(z + (1 if way == 0 else -1), x, y, c),
        )

    def where_to(p, f_side, s_side):
        if p % 2 == 0:
            return (x if f_side == 0 else 1 - x), (y if s_side == 0 else 1 - y)
        return (x if s_side == 0 else 1 - x), (y if f_side == 0 else 1 - y)

    def unit(p, f_side, s_side, core):
        ux, uy = where_to(p, f_side, s_side)
        return fulls[p].at[uy, core, :, ux]

    def first(p):
        ux, uy = where_to(p, 1, 0)
        mine = unit(p, 0, 0, c)
        return remote(mine, mine, f_send.at[p], f_recv.at[p], device(z, ux, uy, c))

    def second(p, f_side):
        ux, uy = where_to(p, 0, 1)
        held = unit(p, f_side, 0, c)
        return remote(
            held, held, s_send.at[p, f_side], s_recv.at[p, f_side], device(z, ux, uy, c)
        )

    def across(p, f_side, s_side):
        held = unit(p, f_side, s_side, c)
        slot = 2 * s_side + f_side
        return remote(
            held, held, c_send.at[p, slot], c_recv.at[p, slot], device(z, x, y, 1 - c)
        )

    owns = []
    for p in range(PIECES):
        own = pltpu.make_async_copy(shards[p], fulls[p].at[y, c, z, x], local.at[p])
        own.start()
        owns.append(own)
    for p in range(PIECES):
        owns[p].wait()

        @pl.when(z < depth - 1)
        def _():
            along_z(p, 0, z).start()

        @pl.when(z > 0)
        def _():
            along_z(p, 1, z).start()

    def z_stage(p):
        def step(s, carry):
            @pl.when(z - s >= 0)
            def _():
                along_z(p, 0, z - s).wait_recv()

                @pl.when(z < depth - 1)
                def _():
                    along_z(p, 0, z - s).start()

            @pl.when(z + s < depth)
            def _():
                along_z(p, 1, z + s).wait_recv()

                @pl.when(z > 0)
                def _():
                    along_z(p, 1, z + s).start()

            return carry

        lax.fori_loop(1, depth, step, 0)
        first(p).start()
        second(p, 0).start()
        across(p, 0, 0).start()

    def f_stage(p):
        first(p).wait_recv()
        second(p, 1).start()
        across(p, 1, 0).start()

    def s_stage(p):
        for f_side in range(2):
            second(p, f_side).wait_recv()
            across(p, f_side, 1).start()

    z_stage(0)
    z_stage(1)
    z_stage(2)
    f_stage(0)
    f_stage(1)
    z_stage(3)
    f_stage(2)
    f_stage(3)
    for p in range(PIECES):
        s_stage(p)
    for p in range(PIECES):
        for slot in range(4):
            across(p, slot % 2, slot // 2).wait()
        first(p).wait_send()
        second(p, 0).wait_send()
        second(p, 1).wait_send()

        def drain(owner, carry):
            @pl.when((owner <= z) & (z < depth - 1))
            def _():
                along_z(p, 0, owner).wait_send()

            @pl.when((owner >= z) & (z > 0))
            def _():
                along_z(p, 1, owner).wait_send()

            return carry

        lax.fori_loop(0, depth, drain, 0)


def gather(shards):
    dp, ctx = lax.axis_size("dp"), lax.axis_size("ctx")
    lead = (ctx // PAIR, PAIR, dp // PAIR, PAIR)
    dma = pltpu.SemaphoreType.DMA
    return pl.pallas_call(
        gather_kernel,
        out_shape=[jax.ShapeDtypeStruct(lead + shard.shape, shard.dtype) for shard in shards],
        in_specs=[pl.BlockSpec(memory_space=pl.ANY)] * PIECES,
        out_specs=[pl.BlockSpec(memory_space=pl.ANY)] * PIECES,
        scratch_shapes=[
            dma((PIECES,)),
            dma((2, PIECES, lead[2])),
            dma((2, PIECES, lead[2])),
            dma((PIECES,)),
            dma((PIECES,)),
            dma((PIECES, 2)),
            dma((PIECES, 2)),
            dma((PIECES, 4)),
            dma((PIECES, 4)),
        ],
        compiler_params=pltpu.CompilerParams(collective_id=0, has_side_effects=True),
        name="weight_gather",
    )(*shards)


def scatter_kernel(*refs):
    grads, sums = refs[:PIECES], refs[PIECES : 2 * PIECES]
    rest = refs[2 * PIECES :]
    locals_, cores, seconds, firsts, lines = (
        rest[i * PIECES : (i + 1) * PIECES] for i in range(5)
    )
    l_sem, z_send, z_recv, f_send, f_recv, s_send, s_recv, c_send, c_recv = rest[5 * PIECES :]
    depth = grads[0].shape[2]
    z, x, y, c = place()

    def sides(p):
        return (x, y) if p % 2 == 0 else (y, x)

    def block(p, f, s, core):
        return grads[p].at[s, core, :, f] if p % 2 == 0 else grads[p].at[f, core, :, s]

    def own(p, f_side, s_side):
        f, s = sides(p)
        f = f if f_side == 0 else 1 - f
        s = s if s_side == 0 else 1 - s
        slot = 2 * s_side + f_side
        return pltpu.make_async_copy(
            block(p, f, s, c), locals_[p].at[slot], l_sem.at[p, slot]
        )

    def across(p, f_side, s_side):
        f, s = sides(p)
        f = f if f_side == 0 else 1 - f
        s = s if s_side == 0 else 1 - s
        slot = 2 * s_side + f_side
        return remote(
            block(p, f, s, 1 - c),
            cores[p].at[slot],
            c_send.at[p, slot],
            c_recv.at[p, slot],
            device(z, x, y, 1 - c),
        )

    def second(p, f_side):
        where = device(z, x, 1 - y, c) if p % 2 == 0 else device(z, 1 - x, y, c)
        return remote(
            cores[p].at[2 + f_side],
            seconds[p].at[f_side],
            s_send.at[p, f_side],
            s_recv.at[p, f_side],
            where,
        )

    def first(p):
        where = device(z, 1 - x, y, c) if p % 2 == 0 else device(z, x, 1 - y, c)
        return remote(seconds[p].at[1], firsts[p], f_send.at[p], f_recv.at[p], where)

    def along_z(p, way, goal, source):
        return remote(
            source,
            lines[p].at[way, goal],
            z_send.at[way, p, goal],
            z_recv.at[way, p, goal],
            device(z + (1 if way == 0 else -1), x, y, c),
        )

    def add(target, source):
        def step(i, carry):
            total = target[i].astype(jnp.float32) + source[i].astype(jnp.float32)
            target[i] = total.astype(jnp.bfloat16)
            return carry

        lax.fori_loop(0, depth, step, 0)

    for p in range(PIECES):
        for slot in (3, 2, 1, 0):
            own(p, slot % 2, slot // 2).start()
    greet(z, x, y, c, depth)
    for p in range(PIECES):
        for slot in (3, 2, 1, 0):
            across(p, slot % 2, slot // 2).start()

    def core_sum(p, slot):
        own(p, slot % 2, slot // 2).wait()
        across(p, slot % 2, slot // 2).wait_recv()
        add(cores[p].at[slot], locals_[p].at[slot])

    def s_stage(p):
        for f_side in (1, 0):
            core_sum(p, 2 + f_side)
            second(p, f_side).start()

    def f_stage(p):
        for f_side in (1, 0):
            core_sum(p, f_side)
            second(p, f_side).wait_recv()
            add(seconds[p].at[f_side], cores[p].at[f_side])
            if f_side == 1:
                first(p).start()

    def pass_on(p, way, goal, has_before):
        @pl.when(has_before)
        def _():
            along_z(p, way, goal, lines[p].at[way, goal]).wait_recv()
            total = lines[p][way, goal].astype(jnp.float32) + firsts[p][goal].astype(jnp.float32)
            lines[p][way, goal] = total.astype(jnp.bfloat16)
            along_z(p, way, goal, lines[p].at[way, goal]).start()

        @pl.when(jnp.logical_not(has_before))
        def _():
            along_z(p, way, goal, firsts[p].at[goal]).start()

    def z_stage(p):
        first(p).wait_recv()
        add(firsts[p], seconds[p].at[0])

        def step(s, carry):
            @pl.when(z < depth - s)
            def _():
                pass_on(p, 0, depth - s, z > 0)

            @pl.when(z > s - 1)
            def _():
                pass_on(p, 1, s - 1, z < depth - 1)

            return carry

        lax.fori_loop(1, depth, step, 0)

    def finish(p):
        sums[p][...] = firsts[p][z].astype(jnp.float32)

        @pl.when(z > 0)
        def _():
            along_z(p, 0, z, lines[p].at[0, z]).wait_recv()
            sums[p][...] += lines[p][0, z].astype(jnp.float32)

        @pl.when(z < depth - 1)
        def _():
            along_z(p, 1, z, lines[p].at[1, z]).wait_recv()
            sums[p][...] += lines[p][1, z].astype(jnp.float32)

    for p in range(PIECES):
        s_stage(p)
    for p in range(PIECES):
        f_stage(p)
        if p > 0:
            z_stage(p - 1)
    z_stage(PIECES - 1)
    for p in range(PIECES):
        finish(p)
    for p in range(PIECES):
        for slot in range(4):
            across(p, slot % 2, slot // 2).wait_send()
        second(p, 0).wait_send()
        second(p, 1).wait_send()
        first(p).wait_send()

        def drain(goal, carry):
            @pl.when(goal > z)
            def _():
                along_z(p, 0, goal, firsts[p].at[goal]).wait_send()

            @pl.when(goal < z)
            def _():
                along_z(p, 1, goal, firsts[p].at[goal]).wait_send()

            return carry

        lax.fori_loop(0, depth, drain, 0)


def scatter(grads):
    depth = grads[0].shape[2]
    dma = pltpu.SemaphoreType.DMA
    shapes = [grad.shape[4:] for grad in grads]

    def slots(lead):
        return [pltpu.VMEM(lead + (depth,) + shape, jnp.bfloat16) for shape in shapes]

    return pl.pallas_call(
        scatter_kernel,
        out_shape=[jax.ShapeDtypeStruct(shape, jnp.float32) for shape in shapes],
        in_specs=[pl.BlockSpec(memory_space=pl.ANY)] * PIECES,
        out_specs=[pl.BlockSpec(memory_space=pltpu.VMEM)] * PIECES,
        scratch_shapes=slots((4,))
        + slots((4,))
        + slots((2,))
        + slots(())
        + slots((2,))
        + [
            dma((PIECES, 4)),
            dma((2, PIECES, depth)),
            dma((2, PIECES, depth)),
            dma((PIECES,)),
            dma((PIECES,)),
            dma((PIECES, 2)),
            dma((PIECES, 2)),
            dma((PIECES, 4)),
            dma((PIECES, 4)),
        ],
        compiler_params=pltpu.CompilerParams(
            collective_id=1, has_side_effects=True, vmem_limit_bytes=58 * 1024 * 1024
        ),
        name="grad_scatter",
    )(*grads)


EXTRA = 8


def fetch(gain_attn, w_query, w_key, w_value, w_out, gain_ffn, w_gate, w_up, w_down):
    rows = w_query.shape[0]
    mixed = jnp.concatenate([w_query, w_key, w_value, w_out], axis=1)
    gains = jnp.pad(
        jnp.stack([gain_attn, gain_ffn]), ((0, EXTRA - 2), (0, mixed.shape[1] - rows))
    )
    full_mixed, full_gate, full_up, full_down = gather(
        [jnp.concatenate([mixed, gains], axis=0), w_gate, w_up, w_down]
    )
    dp, ctx = lax.axis_size("dp"), lax.axis_size("ctx")

    def whole(array):
        array = array.reshape((ctx, dp) + array.shape[4:])
        return jnp.transpose(array, (1, 2, 0, 3)).reshape(dp * array.shape[2], -1)

    full_mixed = full_mixed.reshape((ctx, dp) + full_mixed.shape[4:])
    one = full_mixed[0, :, rows, :rows].reshape(-1)
    two = full_mixed[0, :, rows + 1, :rows].reshape(-1)
    full_mixed = full_mixed[:, :, :rows]
    parts = []
    low = 0
    for weight in (w_query, w_key, w_value, w_out):
        wide = weight.shape[1]
        part = jnp.transpose(full_mixed[..., low : low + wide], (1, 2, 0, 3))
        parts.append(part.reshape(dp * rows, ctx * wide))
        low += wide
    return (*parts, whole(full_gate), whole(full_up), whole(full_down), one, two)


def settle(
    grad_one, grad_query, grad_key, grad_value, grad_out, grad_two, grad_gate, grad_up, grad_down
):
    dp, ctx = lax.axis_size("dp"), lax.axis_size("ctx")
    lead = (ctx // PAIR, PAIR, dp // PAIR, PAIR)

    def blocks(array):
        rows, wide = array.shape[0] // dp, array.shape[1] // ctx
        array = array.astype(jnp.bfloat16).reshape(dp, rows, ctx, wide)
        return jnp.transpose(array, (2, 0, 1, 3))

    mixed = jnp.concatenate(
        [blocks(array) for array in (grad_query, grad_key, grad_value, grad_out)], axis=3
    )
    rows, wide = mixed.shape[2:]
    gains = jnp.stack([grad_one.reshape(dp, rows), grad_two.reshape(dp, rows)], axis=1)
    gains = jnp.pad(gains.astype(jnp.bfloat16), ((0, 0), (0, EXTRA - 2), (0, wide - rows)))
    gains = jnp.broadcast_to(gains[None], (ctx,) + gains.shape)
    mixed = jnp.concatenate([mixed, gains], axis=2)
    pieces = [mixed, blocks(grad_gate), blocks(grad_up), blocks(grad_down)]
    own_mixed, own_gate, own_up, own_down = scatter(
        [piece.reshape(lead + piece.shape[2:]) for piece in pieces]
    )
    cuts = []
    low = 0
    for grad in (grad_query, grad_key, grad_value, grad_out):
        high = low + grad.shape[1] // ctx
        cuts.append(own_mixed[:rows, low:high])
        low = high
    return (
        own_mixed[rows, :rows],
        *cuts,
        own_mixed[rows + 1, :rows],
        own_gate,
        own_up,
        own_down,
    )


def masked_scores(queries, key_block, allowed, factor):
    scores = (
        jnp.einsum("mcgd,mld->mgcl", queries, key_block, preferred_element_type=jnp.float32)
        * factor
    )
    return jnp.where(allowed, scores, -1e30)


def attend(operands, allowed, factor):
    queries, key_block, value_block = operands
    scores = masked_scores(queries, key_block, allowed, factor)
    peak = jnp.max(scores, axis=-1, keepdims=True)
    raised = jnp.exp(scores - peak)
    summed = jnp.sum(raised, axis=-1, keepdims=True)
    shares = (raised / summed).astype(jnp.bfloat16)
    blended = jnp.einsum("mgcl,mld->mcgd", shares, value_block, preferred_element_type=jnp.float32)
    return (blended.astype(jnp.bfloat16), peak + jnp.log(summed))


def attend_back(operands, allowed, factor):
    queries, key_block, value_block, upstream, logsum = operands
    scores = masked_scores(queries, key_block, allowed, factor)
    shares = jnp.exp(scores - logsum)
    d_values = jnp.einsum(
        "mgcl,mcgd->mld", shares.astype(jnp.bfloat16), upstream, preferred_element_type=jnp.float32
    )
    d_shares = jnp.einsum(
        "mcgd,mld->mgcl", upstream, value_block, preferred_element_type=jnp.float32
    )
    row_dot = jnp.sum(d_shares * shares, axis=-1, keepdims=True)
    d_scores = (shares * (d_shares - row_dot)).astype(jnp.bfloat16)
    d_queries = (
        jnp.einsum("mgcl,mld->mcgd", d_scores, key_block, preferred_element_type=jnp.float32)
        * factor
    )
    d_keys = (
        jnp.einsum("mgcl,mcgd->mld", d_scores, queries, preferred_element_type=jnp.float32) * factor
    )
    return (d_queries, d_keys, d_values)


def on_device(
    tokens,
    lengths,
    gain_attn,
    w_query,
    w_key,
    w_value,
    w_out,
    gain_ffn,
    w_gate,
    w_up,
    w_down,
    grad_out,
):
    seq_count, span_len, width = tokens.shape
    groups = lax.axis_size("ctx")
    length = span_len * groups
    ctx_rank = lax.axis_index("ctx")
    batch_size = seq_count
    per_kv = HEADS // KV_HEADS
    query_width = HEADS * HEAD_DIM
    key_width = KV_HEADS * HEAD_DIM
    factor = HEAD_DIM ** (-0.5)
    half_dim = HEAD_DIM // 2
    inverse = THETA ** (-(jnp.arange(half_dim, dtype=jnp.float32) * 2.0 / HEAD_DIM))
    query_pos = ctx_rank * span_len + jnp.arange(span_len, dtype=jnp.int32)
    angles = query_pos.astype(jnp.float32)[:, None] * inverse[None, :]
    cosine = jnp.cos(angles)
    sine_part = jnp.sin(angles)
    cos_query = cosine[:, None, None, :]
    sin_query = sine_part[:, None, None, :]
    cos_key = cosine[:, None, :]
    sin_key = sine_part[:, None, :]
    key_pos = jnp.arange(length, dtype=jnp.int32)
    causal = key_pos[None, :] <= query_pos[:, None]
    rows = batch_size * span_len
    shards = (gain_attn, w_query, w_key, w_value, w_out, gain_ffn, w_gate, w_up, w_down)
    forward_weights = fetch(*shards)
    (
        full_query,
        full_key,
        full_value,
        full_out,
        full_gate,
        full_up,
        full_down,
        full_one,
        full_two,
    ) = forward_weights
    gain_one = full_one.astype(jnp.float32)
    gain_two = full_two.astype(jnp.float32)
    inputs = tokens.astype(jnp.float32).reshape(rows, width)
    valid_len = lengths
    allowed = causal[None, None] & (
        key_pos[None, None, None, :] < valid_len[:, None, None, None]
    )
    normed_attn = rms_scale(inputs, gain_one).astype(jnp.bfloat16)
    queries = product(normed_attn, full_query).reshape(
        batch_size, span_len, KV_HEADS, per_kv, HEAD_DIM
    )
    queries = rotate(queries, cos_query, sin_query).astype(jnp.bfloat16)
    key_own = product(normed_attn, full_key).reshape(batch_size, span_len, KV_HEADS, HEAD_DIM)
    key_own = (
        rotate(key_own, cos_key, sin_key)
        .astype(jnp.bfloat16)
        .reshape(batch_size, span_len, key_width)
    )
    value_own = (
        product(normed_attn, full_value)
        .astype(jnp.bfloat16)
        .reshape(batch_size, span_len, key_width)
    )
    key_all, value_all = (
        lax.all_gather(key_own, "ctx", axis=1, tiled=True),
        lax.all_gather(value_own, "ctx", axis=1, tiled=True),
    )
    head_query = jnp.moveaxis(queries, 2, 0)
    head_key = jnp.moveaxis(key_all.reshape(batch_size, length, KV_HEADS, HEAD_DIM), 2, 0)
    head_value = jnp.moveaxis(value_all.reshape(batch_size, length, KV_HEADS, HEAD_DIM), 2, 0)
    blended, logsum = lax.map(
        partial(attend, allowed=allowed, factor=factor), (head_query, head_key, head_value)
    )
    attended = jnp.moveaxis(blended, 0, 2).reshape(rows, query_width)
    hidden = inputs + product(attended, full_out)
    normed_ffn = rms_scale(hidden, gain_two).astype(jnp.bfloat16)
    gating = product(normed_ffn, full_gate)
    up_proj = product(normed_ffn, full_up)
    inner = silu_gate(gating, up_proj).astype(jnp.bfloat16)
    result = hidden + product(inner, full_down)
    output_all = result.astype(jnp.bfloat16).reshape(batch_size, span_len, width)
    upstream = grad_out.astype(jnp.float32).reshape(rows, width)
    d_down = upstream.astype(jnp.bfloat16)
    grad_down = outer_sum(inner, d_down)
    d_inner = against(d_down, full_down)
    gate_pull = jax.vjp(silu_gate, gating, up_proj)[1]
    d_gating, d_up = gate_pull(d_inner)
    d_gating = d_gating.astype(jnp.bfloat16)
    d_up = d_up.astype(jnp.bfloat16)
    grad_gate = outer_sum(normed_ffn, d_gating)
    grad_up = outer_sum(normed_ffn, d_up)
    d_normed_ffn = against(d_gating, full_gate) + against(d_up, full_up)
    ffn_pull = jax.vjp(rms_scale, hidden, full_two.astype(jnp.float32))[1]
    d_hidden_part, grad_two = ffn_pull(d_normed_ffn)
    d_hidden = upstream + d_hidden_part
    d_attn = d_hidden.astype(jnp.bfloat16)
    grad_out_w = outer_sum(attended, d_attn)
    d_attended = against(d_attn, full_out).astype(jnp.bfloat16)
    head_upstream = jnp.moveaxis(
        d_attended.reshape(batch_size, span_len, KV_HEADS, per_kv, HEAD_DIM), 2, 0
    )
    d_query_h, d_key_h, d_value_h = lax.map(
        partial(attend_back, allowed=allowed, factor=factor),
        (head_query, head_key, head_value, head_upstream, logsum),
    )
    d_key_full = jnp.moveaxis(d_key_h, 0, 2).reshape(batch_size, length, key_width)
    d_value_full = jnp.moveaxis(d_value_h, 0, 2).reshape(batch_size, length, key_width)
    d_key_own, d_value_own = (
        lax.psum_scatter(d_key_full, "ctx", scatter_dimension=1, tiled=True),
        lax.psum_scatter(d_value_full, "ctx", scatter_dimension=1, tiled=True),
    )
    d_query = (
        rotate(jnp.moveaxis(d_query_h, 0, 2), cos_query, -sin_query)
        .astype(jnp.bfloat16)
        .reshape(rows, query_width)
    )
    d_key = (
        rotate(d_key_own.reshape(batch_size, span_len, KV_HEADS, HEAD_DIM), cos_key, -sin_key)
        .astype(jnp.bfloat16)
        .reshape(rows, key_width)
    )
    d_value = d_value_own.astype(jnp.bfloat16).reshape(rows, key_width)
    grad_query = outer_sum(normed_attn, d_query)
    grad_key = outer_sum(normed_attn, d_key)
    grad_value = outer_sum(normed_attn, d_value)
    d_normed_attn = (
        against(d_query, full_query) + against(d_key, full_key) + against(d_value, full_value)
    )
    attn_pull = jax.vjp(rms_scale, inputs, full_one.astype(jnp.float32))[1]
    d_input_part, grad_one = attn_pull(d_normed_attn)
    grads_all = (d_hidden + d_input_part).astype(jnp.bfloat16).reshape(batch_size, span_len, width)
    local_grads = (
        grad_one,
        grad_query,
        grad_key,
        grad_value,
        grad_out_w,
        grad_two,
        grad_gate,
        grad_up,
        grad_down,
    )
    owned = settle(*local_grads)
    return (
        output_all,
        grads_all,
        owned[0],
        owned[1],
        owned[2],
        owned[3],
        owned[4],
        owned[5],
        owned[6],
        owned[7],
        owned[8],
    )


def solution(mesh):
    return jax.shard_map(
        on_device,
        mesh=mesh,
        in_specs=(
            P("dp", "ctx", None),
            P("dp"),
            P("dp"),
            P("dp", "ctx"),
            P("dp", "ctx"),
            P("dp", "ctx"),
            P("dp", "ctx"),
            P("dp"),
            P("dp", "ctx"),
            P("dp", "ctx"),
            P("dp", "ctx"),
            P("dp", "ctx", None),
        ),
        out_specs=(
            P("dp", "ctx", None),
            P("dp", "ctx", None),
            P("dp"),
            P("dp", "ctx"),
            P("dp", "ctx"),
            P("dp", "ctx"),
            P("dp", "ctx"),
            P("dp"),
            P("dp", "ctx"),
            P("dp", "ctx"),
            P("dp", "ctx"),
        ),
        check_vma=False,
    )
```

time: 1470 us -> 753 us (0.51)
  waiting for transfers between devices: 812 us -> 0.62 us
  Pallas kernels: 0 us -> 258 us
  blocking collectives: 196 us -> 0 us
  local copies, waits for them, and re-layouts: 110 us -> 177 us
  matrix products: 276 us -> 239 us
    unnamed x32 -> x4, waiting for transfers between devices: 385 us -> 0.57 us
    all_gather x5 -> x0, waiting for transfers between devices: 261 us -> none  [the longest x1 79.7 us: fetch(): lax.all_gather(col_down, 'dp', axis=0, tiled=True)]
    pallas_call x0 -> x2, Pallas kernels: none -> 258 us  [the longest x1 133 us: scatter(): pl.pallas_call(scatter_kernel, out_shape=[jax.ShapeDtypeStruct(shape, jnp...]
    reduce_scatter x5 -> x0, waiting for transfers between devices: 137 us -> none  [the longest x1 66.3 us: settle(): lax.psum_scatter(sum_out, 'dp', scatter_dimension=0, tiled=True)]
    all_gather x9 -> x0, blocking collectives: 117 us -> none  [the longest x1 32.8 us: fetch(): lax.all_gather(col_value, 'dp', axis=0, tiled=True)]
    reshape x4 -> x20, local copies, waits for them, and re-layouts: 0.68 us -> 108 us  [the longest x12 68.2 us: blocks(): array = array.astype(jnp.bfloat16).reshape(dp, rows, ctx, wide)]
    unnamed x3 -> x0, blocking collectives: 78.7 us -> none
    unnamed x229 -> x108, local copies, waits for them, and re-layouts: 70.8 us -> 37.3 us
  transfers between devices with their start and end apart: 25 -> 4, of which waited for: 17 -> 0; matrix products, arithmetic and copies ran while one was open for 20% -> 28% of each run, Pallas kernels for 0% -> 0%
where the time goes in v1:
time: 753 us; the launch traced here: 743 us
  Pallas kernels  258 us (34%)
  matrix products  239 us (32%)
  local copies, waits for them, and re-layouts  177 us (24%)
  other arithmetic  51.7 us (7%)
  between operations  14.9 us (2%)
    pallas_call x1, Pallas kernels, scatter(): pl.pallas_call(scatter_kernel, out_shape=[jax.ShapeDtypeStruct(shape, jnp...  133 us
    pallas_call x1, Pallas kernels, gather(): pl.pallas_call(gather_kernel, out_shape=[jax.ShapeDtypeStruct(lead + shar...  125 us
    reshape x12, local copies, waits for them, and re-layouts, blocks(): array = array.astype(jnp.bfloat16).reshape(dp, rows, ctx, wide)  68.2 us
    dot_general x7, matrix products, against(): lax.dot_general(former, latter, (((1,), (1,)), ((), ())), preferred_eleme...  53.8 us
    dot_general x7, matrix products, outer_sum(): lax.dot_general(former, latter, (((0,), (0,)), ((), ())), preferred_eleme...  47 us
    unnamed x108, local copies, waits for them, and re-layouts  37.3 us
    dot_general x7, matrix products, product(): return jnp.dot(former, latter, preferred_element_type=jnp.float32)  35.8 us
    dot_general x10, matrix products, masked_scores(): jnp.einsum('mcgd,mld->mgcl', queries, key_block, preferred_element_type=j...  22 us
  transfers between devices with their start and end apart: 4, of which 0 were waited for; matrix products, arithmetic and copies ran while one was open for 28% of the time, Pallas kernels for 0%

profile of v1, /device:TPU:0, one launch (start us, length us, event | category | flops | bytes accessed | tf_op | source)
XLA Modules:
  0.0 742.6 jit_solution(11608994130962562326)
XLA Ops:
  11.4 125.3 %weight_gather.1 = (bf16[2,2,4,2,128,640]{5,4,3,2,1,0:T(8,128)(2,1)}, bf16[2,2,4,2,120,640]{5,4,3,2,1,0:T(8,128)(2,1)}, bf16[2,2,4,2,120,640]{5,4,3,2,1,0:T(8,128)(2,1)}, bf16[2,2,4,2,320,240]{5,4,3,2,1,0:T(8,128)(2,1)}) custom-call(bf16[128,640]{1,0:T(8,128)(2,1)} %pad_maximum_fusion.4.refs_0_, bf16[120,640]{1,0:T(8,128)(2,1)} %refs_1_.1, ...), custom_call_target="tpu_custom_call" | custom-call | tf_op jit(solution)/shard_map/weight_gather/pallas_call | solution.py:225
  160.1 5.2 fusion.158
  182.7 4.8 fusion.96
  189.9 6.3 copy.64
  206.4 6.4 copy.211
  212.9 9.8 %reshape.555 = bf16[2560,960]{1,0:T(8,128)(2,1)} reshape(bf16[8,320,4,240]{3,2,1,0:T(4,128)(2,1)} %bitcast.468) | data formatting | bytes 9830400 | tf_op jit(solution)/shard_map/reshape | solution.py:465
  229.9 40.4 %while.28 = (s32[]{:T(128)}, bf16[5,8,128,3,64]{2,4,3,1,0:T(8,128)(2,1)}, f32[5,8,3,128,1]{3,2,1,4,0:T(4,128)S(1)}, bf16[5,8,512,64]{2,3,1,0:T(8,128)(2,1)}, bf1...) while((s32[]{:T(128)}, ...), condition=%wide.region_4.5_spmd.clone, body=%wide.region_1.4_spmd.clone.sunk | while | flops 422245376 | bytes 22988904 | solution.py:640
  278.3 8.4 %fusion.162 = f32[1024,2560]{1,0:T(8,128)} fusion(bf16[1024,960]{0,1:T(8,128)(2,1)S(1)} %multiply_convert_fusion.1, bf16[960,2560]{1,0:T(8,128)(2,1)S(1)} %bitcast.501), kind=kOutput, calls=%fused_computation.216 | convolution fusion | flops 5033164800 | bytes 17367040 | tf_op jit(solution)/shard_map/dot_general | solution.py:22
  286.7 8.3 %fusion.163 = f32[1024,2560]{1,0:T(8,128)} fusion(bf16[1024,960]{0,1:T(8,128)(2,1)S(1)} %multiply_convert_fusion.1, bf16[960,2560]{1,0:T(8,128)(2,1)S(1)} %bitcast.497), kind=kOutput, calls=%fused_computation.217 | convolution fusion | flops 5033164800 | bytes 17367040 | tf_op jit(solution)/shard_map/dot_general | solution.py:22
  295.0 18.9 %fusion.67 = (bf16[1024,2560]{1,0:T(8,128)(2,1)}, bf16[1024,2560]{1,0:T(8,128)(2,1)}, bf16[1024,2560]{1,0:T(8,128)(2,1)}) fusion(f32[1024,2560]{1,0:T(8,128)} %fusion.162, f32[1024,2560]{1,0:T(8,128)} %fusion.163, bf16[2560,960]{1,0:T(8,128)(2,1)} %reshape.555, bf16[8,128,960]{1,2,0:T(8,128)(2,1)S(1)} %copy-done), kind=kOutput, calls=%fused_computation.75 | convolution fusion | flops 5075107840 | bytes 43581440 | tf_op jit(solution)/shard_map/dot_general | solution.py:26
  314.0 8.8 %fusion.164 = f32[1024,960]{0,1:T(8,128)S(1)} fusion(bf16[1024,2560]{1,0:T(8,128)(2,1)} %get-tuple-element.279, bf16[960,2560]{1,0:T(8,128)(2,1)} %bitcast.498), kind=kOutput, calls=%fused_computation.218 | convolution fusion | flops 5033164800 | bytes 14090240 | tf_op jit(solution)/shard_map/dot_general | solution.py:26
  322.8 8.2 %multiply_reduce_fusion = (bf16[960]{0:T(1024)(128)(2,1)S(1)}, f32[1024]{0:T(1024)S(1)}, f32[1024,960]{0,1:T(8,128)S(1)}) fusion(f32[1024,960]{0,1:T(8,128)S(1)} %copy-done.4, f32[1024]{0:T(1024)S(1)} %fusion.151, f32[960]{0:T(1024)S(1)} %reshape.577, f32[1024,960]{0,1:T(8,128)S(1)} %fusion.164, bf16[1024,2560]{1,0:T(8,128)(2,1)S(1)} %copy-done.32, ...), kind=kOutput, calls=%fused_computation.102 | convolution fusion | flops 5040044032 | bytes 21968512 | tf_op jit(solution)/shard_map/dot_general | solution.py:26
  337.3 87.0 %while.29 = (s32[]{:T(128)}, f32[5,8,128,3,64]{2,4,3,0,1:T(8,128)}, f32[5,8,512,64]{2,3,0,1:T(8,128)}, f32[5,8,512,64]{2,3,0,1:T(8,128)}, bf16[5,8,512,64]{2,3,1...) while((s32[]{:T(128)}, f32[5,8,128,3,64]{2,4,3,0,1:T(8,128)}, ...), condition=%wide.region_9.10_spmd.clone, body=%wide.region_7.9_spmd.clone.sunk | while | flops 1031205888 | bytes 55473280 | solution.py:671
  431.1 7.0 fusion.102
  438.2 6.2 reshape.568
  444.4 5.7 fusion.105
  450.1 6.0 reshape.565
  456.1 9.7 %convolution_convert_fusion.2 = bf16[960,2560]{1,0:T(8,128)(2,1)} fusion(bf16[1024,960]{0,1:T(8,128)(2,1)} %copy-done.13, bf16[1024,2560]{1,0:T(8,128)(2,1)} %get-tuple-element.279), kind=kOutput, calls=%fused_computation.86 | convolution fusion | flops 5035622400 | bytes 12124160 | tf_op jit(solution)/shard_map/dot_general | solution.py:32
  465.9 9.3 %reshape.570 = bf16[8,120,4,640]{3,2,1,0:T(4,128)(2,1)} reshape(bf16[960,2560]{1,0:T(8,128)(2,1)} %convolution_convert_fusion.2) | data formatting | bytes 9830400 | tf_op jit(solution)/shard_map/reshape | solution.py:489
  475.2 5.3 copy.84
  480.5 10.2 %convolution_convert_fusion.1 = bf16[960,2560]{1,0:T(8,128)(2,1)} fusion(bf16[1024,960]{0,1:T(8,128)(2,1)S(1)} %copy-done.14, bf16[1024,2560]{1,0:T(8,128)(2,1)} %get-tuple-element.278), kind=kOutput, calls=%fused_computation.85 | convolution fusion | flops 5035622400 | bytes 12124160 | tf_op jit(solution)/shard_map/dot_general | solution.py:32
  490.8 9.4 %reshape.572 = bf16[8,120,4,640]{3,2,1,0:T(4,128)(2,1)} reshape(bf16[960,2560]{1,0:T(8,128)(2,1)} %convolution_convert_fusion.1) | data formatting | bytes 9830400 | tf_op jit(solution)/shard_map/reshape | solution.py:489
  500.2 5.2 copy.85
  505.4 9.7 %convolution_convert_fusion = bf16[2560,960]{0,1:T(8,128)(2,1)} fusion(bf16[1024,2560]{1,0:T(8,128)(2,1)} %get-tuple-element.280, bf16[8,128,960]{1,2,0:T(8,128)(2,1)S(1)} %copy-done), kind=kOutput, calls=%fused_computation.84 | convolution fusion | flops 5035622400 | bytes 12124160 | tf_op jit(solution)/shard_map/dot_general | solution.py:32
  515.0 10.0 %reshape.589 = bf16[8,320,4,240]{1,0,3,2:T(8,128)(2,1)} reshape(bf16[2560,960]{0,1:T(8,128)(2,1)} %convolution_convert_fusion) | data formatting | bytes 9830400 | tf_op jit(solution)/shard_map/reshape | solution.py:489
  525.0 8.7 %copy.105 = bf16[8,320,4,240]{3,2,1,0:T(4,128)(2,1)} copy(bf16[8,320,4,240]{1,0,3,2:T(8,128)(2,1)} %reshape.589) | data formatting | bytes 9830400 | tf_op jit(solution)/shard_map/reshape | solution.py:489
  533.7 6.0 copy.87
  548.3 6.7 fusion.78
  562.0 8.1 %fusion.77 = (bf16[960]{0:T(1024)(128)(2,1)S(1)}, f32[1024]{0:T(1024)S(1)}, f32[1024,960]{0,1:T(8,128)}) fusion(f32[1024]{0:T(1024)S(1)} %bitcast_rsqrt_fusion, f32[960]{0:T(1024)S(1)} %copy-done.28, bf16[960,320]{0,1:T(8,128)(2,1)S(1)} %copy-done.9, f32[1024,960]{0,1:T(8,128)} %fusion.82, f32[1024,960]{0,1:T(8,128)} %fusion.132, ...), kind=kOutput, calls=%fused_computation.101 | convolution fusion | flops 638318656 | bytes 15701632 | tf_op jit(solution)/shard_map/dot_general | solution.py:26
  581.2 7.5 %pad_maximum_fusion = bf16[4,8,128,640]{3,2,1,0:T(8,128)(2,1)} fusion(bf16[4,8,8,640]{3,2,1,0:T(8,128)(2,1)S(1)} %broadcast_in_dim.91, bf16[4,8,120,240]{3,2,1,0:T(8,128)(2,1)} %get-tuple-element.306, bf16[4,8,120,80]{3,2,1,0:T(8,128)(2,1)S(1)} %bitcast.505, bf16[4,8,120,80]{3,2,1,0:T(8,128)(2,1)} %bitcast.506, bf16[4,8,120,240]{3,2,1,0:T(8,128)(2,1)} %get-tuple-element.307), kind=kLoop, calls=%fused_computation.87 | loop fusion | flops 26214400 | bytes 10485760 | tf_op jit(solution)/shard_map/concatenate | solution.py:499
  588.7 132.7 %grad_scatter.1 = (f32[128,640]{1,0:T(8,128)}, f32[120,640]{1,0:T(8,128)}, f32[120,640]{1,0:T(8,128)}, f32[320,240]{1,0:T(8,128)}) custom-call(bf16[2,2,4,2,128,640]{5,4,3,2,1,0:T(8,128)(2,1)} %bitcast.471, bf16[2,2,4,2,120,640]{5,4,3,2,1,0:T(8,128)(2,1)} %bitcast.472, bf16[2,2,4,2,120,640]{5,4,3,2,1,0:T(8,128)(2,1)} %bitcast.473, ...), custom_call_target="tpu_custom_call" | custom-call | tf_op jit(solution)/shard_map/grad_scatter/pallas_call | solution.py:421
  726.9 6.5 copy_bitcast_fusion.1
  (255 shorter events, 246.3 us)
Async XLA Ops:
  7.2 287.9 %copy-start = (bf16[8,128,960]{1,2,0:T(8,128)(2,1)S(1)}, bf16[8,128,960]{1,2,0:T(8,128)(2,1)}, u32[]{:S(2)}) copy-start(bf16[8,128,960]{1,2,0:T(8,128)(2,1)} %param.27) | copy-start | bytes 5898244
  7.2 215.6 %all-gather.3.cloned.1.call-start = ((), (), s32[]{:S(2)}) async-start(), calls=%async_computation.2 | async-start | bytes 3276800 | tf_op jit(solution)/shard_map/all_gather | solution.py:635
  146.1 36.6 %copy-start.27 = (f32[960]{0:T(1024)}, f32[960]{0:T(1024)S(1)}, u32[]{:S(2)}) copy-start(f32[960]{0:T(1024)S(1)} %reshape.576) | copy-start | bytes 11524
  148.7 34.0 %copy-start.29 = (f32[8,128]{1,0:T(8,128)}, f32[8,128]{1,0:T(8,128)S(1)}, u32[]{:S(2)}) copy-start(f32[8,128]{1,0:T(8,128)S(1)} %fusion.152) | copy-start | bytes 12292
  152.4 74.0 %all-gather.5.cloned.1.call-start = ((), (), s32[]{:S(2)}) async-start(), calls=%async_computation.3 | async-start | bytes 3276800 | tf_op jit(solution)/shard_map/all_gather | solution.py:634
  155.4 4.6 copy-start.10
  156.3 31.2 %copy-start.19 = (f32[128,32]{0,1:T(8,128)}, f32[128,32]{0,1:T(8,128)S(1)}, u32[]{:S(2)}) copy-start(f32[128,32]{0,1:T(8,128)S(1)} %get-tuple-element.301) | copy-start | bytes 49156
  160.0 395.0 %reduce-scatter.3.cloned.1.call-start = ((), (), s32[]{:S(2)}) async-start(), calls=%async_computation.4 | async-start | bytes 6553600 | tf_op jit(solution)/shard_map/reduce_scatter | solution.py:678
  189.8 9.4 %slice-start.4 = ((s8[4915200]{0:T(1024)(128)(4,1)}), s8[4194304]{0:T(1024)(128)(4,1)S(1)}, s32[]{:S(2)}) async-start(s8[4915200]{0:T(1024)(128)(4,1)} %bitcast.490), calls=%async_computation.10 | async-start | bytes 8388608
  199.2 7.2 slice-start.2
  212.9 9.8 %copy-start.31 = (s32[8]{0:T(128)S(1)}, s32[8]{0:T(128)}, u32[]{:S(2)}) copy-start(s32[8]{0:T(128)} %param.17) | copy-start | bytes 100
  273.7 4.6 slice-start.8
  277.9 8.8 %slice-start.6 = ((s8[4915200]{0:T(1024)(128)(4,1)}), s8[720896]{0:T(1024)(128)(4,1)S(1)}, s32[]{:S(2)}) async-start(s8[4915200]{0:T(1024)(128)(4,1)} %bitcast.495), calls=%async_computation.12 | async-start | bytes 1441792
  278.3 8.4 %copy-start.13 = (bf16[1024,960]{0,1:T(8,128)(2,1)}, bf16[1024,960]{0,1:T(8,128)(2,1)S(1)}, u32[]{:S(2)}) copy-start(bf16[1024,960]{0,1:T(8,128)(2,1)S(1)} %multiply_convert_fusion.1) | copy-start | bytes 5898244
  278.3 8.4 %slice-start.7 = ((s8[4915200]{0:T(1024)(128)(4,1)}), s8[4194304]{0:T(1024)(128)(4,1)S(1)}, s32[]{:S(2)}) async-start(s8[4915200]{0:T(1024)(128)(4,1)} %bitcast.495), calls=%async_computation.13 | async-start | bytes 8388608
  314.0 8.8 %copy-start.4 = (f32[1024,960]{0,1:T(8,128)S(1)}, f32[1024,960]{0,1:T(8,128)}, u32[]{:S(2)}) copy-start(f32[1024,960]{0,1:T(8,128)} %copy-done.3) | copy-start | bytes 11796484
  314.0 8.8 %copy-start.32 = (bf16[1024,2560]{1,0:T(8,128)(2,1)S(1)}, bf16[1024,2560]{1,0:T(8,128)(2,1)}, u32[]{:S(2)}) copy-start(bf16[1024,2560]{1,0:T(8,128)(2,1)} %get-tuple-element.278) | copy-start | bytes 15728644
  424.4 137.7 %reduce-scatter.5.cloned.1.call-start = ((), (), s32[]{:S(2)}) async-start(), calls=%async_computation.5 | async-start | bytes 6553600 | tf_op jit(solution)/shard_map/reduce_scatter | solution.py:679
  438.2 6.2 copy-start.28
  438.2 6.3 copy-start.30
  475.2 5.3 copy-start.14
  533.7 6.0 copy-start.7
  533.7 6.0 copy-start.8
  533.7 8.5 %copy-start.18 = (bf16[8,128,5,3,64]{1,0,4,3,2:T(8,128)(2,1)S(1)}, bf16[8,128,5,3,64]{1,0,4,3,2:T(8,128)(2,1)}, u32[]{:S(2)}) copy-start(bf16[8,128,5,3,64]{1,0,4,3,2:T(8,128)(2,1)} %copy.74) | copy-start | bytes 5898244
  539.6 6.9 slice-start
  539.6 6.9 slice-start.10
  542.2 5.5 copy-start.5
  542.2 5.7 slice-start.1
  542.2 6.0 slice-start.11
  726.9 6.5 copy-start.23
  726.9 7.2 copy-start.22
  726.9 7.9 %copy-start.21 = (f32[320,240]{1,0:T(8,128)S(1)}, f32[320,240]{1,0:T(8,128)}, u32[]{:S(2)}) copy-start(f32[320,240]{1,0:T(8,128)} %get-tuple-element.518) | copy-start | bytes 921604
  (17 other events, 37.8 us)
Sparse Core Ops, SparseCore 0:
  152.5 23.9 all-gather.2
  178.0 25.9 all-gather.4
  424.5 49.4 reduce-scatter.2
  476.5 51.3 reduce-scatter.4

commit v2 on v1

--- a/solution.py
+++ b/solution.py
@@ -460,51 +460,58 @@
     )
     dp, ctx = lax.axis_size("dp"), lax.axis_size("ctx")
 
-    def whole(array):
-        array = array.reshape((ctx, dp) + array.shape[4:])
-        return jnp.transpose(array, (1, 2, 0, 3)).reshape(dp * array.shape[2], -1)
-
-    full_mixed = full_mixed.reshape((ctx, dp) + full_mixed.shape[4:])
-    one = full_mixed[0, :, rows, :rows].reshape(-1)
-    two = full_mixed[0, :, rows + 1, :rows].reshape(-1)
-    full_mixed = full_mixed[:, :, :rows]
+    def stacked(array):
+        return array.reshape(ctx, dp * array.shape[4], array.shape[5])
+
+    def beside(array):
+        return jnp.concatenate([array[block] for block in range(ctx)], axis=1)
+
+    corner = full_mixed.reshape((ctx, dp) + full_mixed.shape[4:])[0]
+    one = corner[:, rows, :rows].reshape(-1)
+    two = corner[:, rows + 1, :rows].reshape(-1)
+    blocks = stacked(full_mixed[:, :, :, :, :rows])
     parts = []
     low = 0
     for weight in (w_query, w_key, w_value, w_out):
-        wide = weight.shape[1]
-        part = jnp.transpose(full_mixed[..., low : low + wide], (1, 2, 0, 3))
-        parts.append(part.reshape(dp * rows, ctx * wide))
-        low += wide
-    return (*parts, whole(full_gate), whole(full_up), whole(full_down), one, two)
-
-
-def settle(
-    grad_one, grad_query, grad_key, grad_value, grad_out, grad_two, grad_gate, grad_up, grad_down
-):
+        high = low + weight.shape[1]
+        parts.append(beside(blocks[:, :, low:high]))
+        low = high
+    return (*parts, beside(stacked(full_gate)), beside(stacked(full_up)), beside(stacked(full_down)), one, two)
+
+
+def settle(grad_one, grad_two, mixed_pairs, gate_pair, up_pair, down_pair):
     dp, ctx = lax.axis_size("dp"), lax.axis_size("ctx")
     lead = (ctx // PAIR, PAIR, dp // PAIR, PAIR)
 
-    def blocks(array):
-        rows, wide = array.shape[0] // dp, array.shape[1] // ctx
-        array = array.astype(jnp.bfloat16).reshape(dp, rows, ctx, wide)
-        return jnp.transpose(array, (2, 0, 1, 3))
-
-    mixed = jnp.concatenate(
-        [blocks(array) for array in (grad_query, grad_key, grad_value, grad_out)], axis=3
-    )
+    def blocks(pairs):
+        made = []
+        for block in range(ctx):
+            columns = []
+            for former, latters in pairs:
+                cuts = []
+                for latter in latters:
+                    wide = latter.shape[1] // ctx
+                    cuts.append(latter[:, block * wide : (block + 1) * wide])
+                latter = cuts[0] if len(cuts) == 1 else jnp.concatenate(cuts, axis=1)
+                columns.append(outer_sum(former, latter).astype(jnp.bfloat16))
+            made.append(columns[0] if len(columns) == 1 else jnp.concatenate(columns, axis=1))
+        height, wide = made[0].shape
+        return jnp.stack(made).reshape(ctx, dp, height // dp, wide)
+
+    mixed = blocks(mixed_pairs)
     rows, wide = mixed.shape[2:]
     gains = jnp.stack([grad_one.reshape(dp, rows), grad_two.reshape(dp, rows)], axis=1)
     gains = jnp.pad(gains.astype(jnp.bfloat16), ((0, 0), (0, EXTRA - 2), (0, wide - rows)))
     gains = jnp.broadcast_to(gains[None], (ctx,) + gains.shape)
     mixed = jnp.concatenate([mixed, gains], axis=2)
-    pieces = [mixed, blocks(grad_gate), blocks(grad_up), blocks(grad_down)]
+    pieces = [mixed, blocks([gate_pair]), blocks([up_pair]), blocks([down_pair])]
     own_mixed, own_gate, own_up, own_down = scatter(
         [piece.reshape(lead + piece.shape[2:]) for piece in pieces]
     )
     cuts = []
     low = 0
-    for grad in (grad_query, grad_key, grad_value, grad_out):
-        high = low + grad.shape[1] // ctx
+    for latter in (*mixed_pairs[0][1], *mixed_pairs[1][1]):
+        high = low + latter.shape[1] // ctx
         cuts.append(own_mixed[:rows, low:high])
         low = high
     return (
@@ -650,20 +657,16 @@
     output_all = result.astype(jnp.bfloat16).reshape(batch_size, span_len, width)
     upstream = grad_out.astype(jnp.float32).reshape(rows, width)
     d_down = upstream.astype(jnp.bfloat16)
-    grad_down = outer_sum(inner, d_down)
     d_inner = against(d_down, full_down)
     gate_pull = jax.vjp(silu_gate, gating, up_proj)[1]
     d_gating, d_up = gate_pull(d_inner)
     d_gating = d_gating.astype(jnp.bfloat16)
     d_up = d_up.astype(jnp.bfloat16)
-    grad_gate = outer_sum(normed_ffn, d_gating)
-    grad_up = outer_sum(normed_ffn, d_up)
     d_normed_ffn = against(d_gating, full_gate) + against(d_up, full_up)
     ffn_pull = jax.vjp(rms_scale, hidden, full_two.astype(jnp.float32))[1]
     d_hidden_part, grad_two = ffn_pull(d_normed_ffn)
     d_hidden = upstream + d_hidden_part
     d_attn = d_hidden.astype(jnp.bfloat16)
-    grad_out_w = outer_sum(attended, d_attn)
     d_attended = against(d_attn, full_out).astype(jnp.bfloat16)
     head_upstream = jnp.moveaxis(
         d_attended.reshape(batch_size, span_len, KV_HEADS, per_kv, HEAD_DIM), 2, 0
@@ -689,27 +692,20 @@
         .reshape(rows, key_width)
     )
     d_value = d_value_own.astype(jnp.bfloat16).reshape(rows, key_width)
-    grad_query = outer_sum(normed_attn, d_query)
-    grad_key = outer_sum(normed_attn, d_key)
-    grad_value = outer_sum(normed_attn, d_value)
     d_normed_attn = (
         against(d_query, full_query) + against(d_key, full_key) + against(d_value, full_value)
     )
     attn_pull = jax.vjp(rms_scale, inputs, full_one.astype(jnp.float32))[1]
     d_input_part, grad_one = attn_pull(d_normed_attn)
     grads_all = (d_hidden + d_input_part).astype(jnp.bfloat16).reshape(batch_size, span_len, width)
-    local_grads = (
+    owned = settle(
         grad_one,
-        grad_query,
-        grad_key,
-        grad_value,
-        grad_out_w,
         grad_two,
-        grad_gate,
-        grad_up,
-        grad_down,
-    )
-    owned = settle(*local_grads)
+        [(normed_attn, (d_query, d_key, d_value)), (attended, (d_attn,))],
+        (normed_ffn, (d_gating,)),
+        (normed_ffn, (d_up,)),
+        (inner, (d_down,)),
+    )
     return (
         output_all,
         grads_all,

time: 753 us -> 714 us (0.948)
  local copies, waits for them, and re-layouts: 177 us -> 94.7 us
  waiting for transfers between devices: 0.62 us -> 26.3 us
  other arithmetic: 51.7 us -> 65.2 us
    reshape x20 -> x1, local copies, waits for them, and re-layouts: 108 us -> 1.6 us  [on_device(): upstream = grad_out.astype(jnp.float32).reshape(rows, width)]
    squeeze x0 -> x6, local copies, waits for them, and re-layouts: none -> 19 us  [the longest x5 17.5 us: beside(): return jnp.concatenate([array[block] for block in range(ctx)], axis=1)]
    reduce_scatter x1, waiting for transfers between devices: 0.01 us -> 15.8 us  [on_device(): lax.psum_scatter(d_value_full, 'ctx', scatter_dimension=1, tiled=True)]
    all_gather x1, waiting for transfers between devices: 0.01 us -> 10.5 us  [on_device(): lax.all_gather(key_own, 'ctx', axis=1, tiled=True)]
    transpose x2 -> x0, local copies, waits for them, and re-layouts: 8.5 us -> none  [blocks(): return jnp.transpose(array, (2, 0, 1, 3))]
    another operation x0 -> x1, local copies, waits for them, and re-layouts: none -> 8 us  [blocks(): return jnp.stack(made).reshape(ctx, dp, height // dp, wide)]
    dot_general x7 -> x20, matrix products: 47 us -> 41.3 us  [outer_sum(): lax.dot_general(former, latter, (((0,), (0,)), ((), ())), preferred_eleme...]
    unnamed x108 -> x202, local copies, waits for them, and re-layouts: 37.3 us -> 31.8 us
  transfers between devices with their start and end apart: 4 -> 4, of which waited for: 0 -> 2; matrix products, arithmetic and copies ran while one was open for 28% -> 17% of each run, Pallas kernels for 0% -> 0%
where the time goes in v2:
time: 714 us; the launch traced here: 705 us
  Pallas kernels  258 us (36%)
  matrix products  243 us (34%)
  local copies, waits for them, and re-layouts  94.7 us (13%)
  other arithmetic  65.2 us (9%)
  waiting for transfers between devices  26.3 us (4%)
  between operations  15.6 us (2%)
    pallas_call x1, Pallas kernels, scatter(): pl.pallas_call(scatter_kernel, out_shape=[jax.ShapeDtypeStruct(shape, jnp...  133 us
    pallas_call x1, Pallas kernels, gather(): pl.pallas_call(gather_kernel, out_shape=[jax.ShapeDtypeStruct(lead + shar...  125 us
    dot_general x7, matrix products, against(): lax.dot_general(former, latter, (((1,), (1,)), ((), ())), preferred_eleme...  57.8 us
    dot_general x20, matrix products, outer_sum(): lax.dot_general(former, latter, (((0,), (0,)), ((), ())), preferred_eleme...  41.3 us
    dot_general x7, matrix products, product(): return jnp.dot(former, latter, preferred_element_type=jnp.float32)  41.2 us
    unnamed x202, local copies, waits for them, and re-layouts  31.8 us
    dot_general x10, matrix products, masked_scores(): jnp.einsum('mcgd,mld->mgcl', queries, key_block, preferred_element_type=j...  22 us
    dot_general x5, matrix products, attend_back(): jnp.einsum('mgcl,mcgd->mld', shares.astype(jnp.bfloat16), upstream, prefe...  18.8 us
  transfers between devices with their start and end apart: 4, of which 2 were waited for; matrix products, arithmetic and copies ran while one was open for 17% of the time, Pallas kernels for 0%

profile of v2, /device:TPU:0, one launch (start us, length us, event | category | flops | bytes accessed | tf_op | source)
XLA Modules:
  0.0 704.8 jit_solution(14778197167321958986)
XLA Ops:
  11.4 125.3 %weight_gather.1 = (bf16[2,2,4,2,128,640]{5,4,3,2,1,0:T(8,128)(2,1)}, bf16[2,2,4,2,120,640]{5,4,3,2,1,0:T(8,128)(2,1)}, bf16[2,2,4,2,120,640]{5,4,3,2,1,0:T(8,128)(2,1)}, bf16[2,2,4,2,320,240]{5,4,3,2,1,0:T(8,128)(2,1)}) custom-call(bf16[128,640]{1,0:T(8,128)(2,1)} %pad_maximum_fusion.27.refs_0_, bf16[120,640]{1,0:T(8,128)(2,1)} %refs_1_.1, ...), custom_call_target="tpu_custom_call" | custom-call | tf_op jit(solution)/shard_map/weight_gather/pallas_call | solution.py:225
  136.7 5.0 slice.244
  158.3 4.5 slice_bitcast_fusion.16
  166.4 4.0 copy.60
  170.4 4.5 fusion.92
  177.5 4.8 slice_bitcast_fusion.12
  188.9 4.0 copy.61
  192.9 10.5 %all-gather.5.cloned.1.call-done = bf16[8,512,320]{1,2,0:T(8,128)(2,1)} async-done(((bf16[8,128,320]{1,2,0:T(8,128)(2,1)}), bf16[8,512,320]{1,2,0:T(8,128)(2,1)}) %all-gather.5.cloned.1.call-update) | async-done | bytes 2621456 | tf_op jit(solution)/shard_map/all_gather | solution.py:641
  206.9 40.7 %while.28 = (s32[]{:T(128)}, bf16[5,8,128,3,64]{2,4,3,1,0:T(8,128)(2,1)}, f32[5,8,3,128,1]{3,2,1,4,0:T(4,128)S(1)}, bf16[5,8,512,64]{2,3,1,0:T(8,128)(2,1)}, bf1...) while((s32[]{:T(128)}, ...), condition=%wide.region_4.5_spmd.clone, body=%wide.region_1.4_spmd.clone.sunk | while | flops 422245376 | bytes 22988904 | solution.py:647
  219.3 3.6 fusion.260
  227.4 3.6 fusion.260
  258.7 8.7 %fusion.135 = f32[1024,2560]{1,0:T(8,128)} fusion(bf16[1024,960]{0,1:T(8,128)(2,1)S(1)} %multiply_convert_fusion.1, bf16[960,640]{1,0:T(8,128)(2,1)S(1)} %copy-done.45, bf16[960,640]{1,0:T(8,128)(2,1)S(1)} %copy-done.46, bf16[960,640]{1,0:T(8,128)(2,1)S(1)} %copy-done.47, bf16[960,640]{1,0:T(8,128)(2,1)S(1)} %copy-done.44), kind=kOutput, calls=%fused_computation.208 | convolution fusion | flops 5052825600 | bytes 17367040 | tf_op jit(solution)/shard_map/dot_general | solution.py:22
  267.4 8.7 %fusion.133 = f32[1024,2560]{1,0:T(8,128)} fusion(bf16[1024,960]{0,1:T(8,128)(2,1)S(1)} %multiply_convert_fusion.1, bf16[960,640]{1,0:T(8,128)(2,1)S(1)} %copy-done.38, bf16[960,640]{1,0:T(8,128)(2,1)S(1)} %copy-done.40, bf16[960,640]{1,0:T(8,128)(2,1)S(1)} %copy-done.42, bf16[960,640]{1,0:T(8,128)(2,1)S(1)} %copy-done.36), kind=kOutput, calls=%fused_computation.206 | convolution fusion | flops 5052825600 | bytes 17367040 | tf_op jit(solution)/shard_map/dot_general | solution.py:22
  276.1 20.0 %fusion.67 = (bf16[1024,2560]{1,0:T(8,128)(2,1)}, bf16[1024,2560]{1,0:T(8,128)(2,1)}, bf16[1024,2560]{1,0:T(8,128)(2,1)}) fusion(f32[1024,2560]{1,0:T(8,128)} %fusion.135, f32[1024,2560]{1,0:T(8,128)} %fusion.133, bf16[2560,240]{1,0:T(8,128)(2,1)} %get-tuple-element.282, bf16[2560,240]{1,0:T(8,128)(2,1)} %get-tuple-element.283, ...), kind=kOutput, calls=%fused_computation.75 | convolution fusion | flops 5094768640 | bytes 43581440 | tf_op jit(solution)/shard_map/dot_general | solution.py:26
  296.1 10.4 %fusion.134 = f32[1024,960]{0,1:T(8,128)} fusion(bf16[1024,2560]{1,0:T(8,128)(2,1)} %get-tuple-element.279, bf16[960,640]{1,0:T(8,128)(2,1)} %get-tuple-element.286, bf16[960,640]{1,0:T(8,128)(2,1)} %get-tuple-element.287, bf16[960,640]{1,0:T(8,128)(2,1)} %get-tuple-element.288, bf16[960,640]{1,0:T(8,128)(2,1)} %get-tuple-element.285), kind=kOutput, calls=%fused_computation.207 | convolution fusion | flops 5052825600 | bytes 14090240 | tf_op jit(solution)/shard_map/dot_general | solution.py:26
  306.6 9.5 %multiply_reduce_fusion = (bf16[960]{0:T(1024)(128)(2,1)S(1)}, f32[1024]{0:T(1024)S(1)}, f32[1024,960]{0,1:T(8,128)S(1)}) fusion(f32[1024,960]{0,1:T(8,128)S(1)} %get-tuple-element.339, f32[1024]{0:T(1024)S(1)} %fusion.181, f32[960]{0:T(1024)S(1)} %reshape.457, f32[1024,960]{0,1:T(8,128)} %fusion.134, bf16[1024,2560]{1,0:T(8,128)(2,1)} %get-tuple-element.278, ...), kind=kOutput, calls=%fused_computation.102 | convolution fusion | flops 5059704832 | bytes 21968512 | tf_op jit(solution)/shard_map/dot_general | solution.py:26
  323.2 87.1 %while.29 = (s32[]{:T(128)}, f32[5,8,128,3,64]{2,4,3,0,1:T(8,128)}, f32[5,8,512,64]{2,3,0,1:T(8,128)}, f32[5,8,512,64]{2,3,0,1:T(8,128)}, bf16[5,8,512,64]{2,3,1...) while((s32[]{:T(128)}, f32[5,8,128,3,64]{2,4,3,0,1:T(8,128)}, ...), condition=%wide.region_9.10_spmd.clone, body=%wide.region_7.9_spmd.clone.sunk | while | flops 1031205888 | bytes 55473280 | solution.py:674
  337.1 3.8 fusion.274
  354.5 3.7 fusion.274
  371.8 3.7 fusion.274
  389.2 3.8 fusion.274
  406.5 3.8 fusion.274
  424.3 4.2 fusion.79
  428.6 4.8 fusion.78
  439.1 8.0 %copy.86 = bf16[4,2560,240]{2,1,0:T(8,128)(2,1)} copy(bf16[4,2560,240]{1,2,0:T(8,128)(2,1)} %pad_maximum_fusion.6) | data formatting | bytes 9830400 | tf_op jit(solution)/shard_map/stack | solution.py:499
  477.3 4.1 fusion.166
  481.5 12.3 %fusion.80 = bf16[120,8,8,128]{3,2,1,0:T(8,128)(2,1)} fusion(f32[1024,960]{0,1:T(8,128)S(1)} %copy-done.2, bf16[1024,2560]{1,0:T(8,128)(2,1)} %get-tuple-element.280, bf16[2560,240]{1,0:T(8,128)(2,1)} %get-tuple-element.282, bf16[2560,240]{1,0:T(8,128)(2,1)} %get-tuple-element.283, bf16[2560,240]{1,0:T(8,128)(2,1)} %get-tuple-element.284, ...), kind=kOutput, calls=%fused_computation.118 | convolution fusion | flops 5054791680 | bytes 16056320 | tf_op jit(solution)/shard_map/dot_general | solution.py:22
  500.1 15.8 %reduce-scatter.5.cloned.1.call-done = f32[8,128,320]{1,2,0:T(8,128)} async-done(((f32[8,512,320]{1,2,0:T(8,128)}), f32[8,128,320]{1,2,0:T(8,128)}) %reduce-scatter.5.cloned.1.call-update) | async-done | bytes 1310736 | tf_op jit(solution)/shard_map/reduce_scatter | solution.py:682
  515.9 8.3 %multiply_reduce_fusion.1 = (bf16[960]{0:T(1024)(128)(2,1)S(1)}, f32[1024]{0:T(1024)S(1)}, f32[1024,960]{0,1:T(8,128)}) fusion(f32[1024]{0:T(1024)S(1)} %copy-done.76, f32[960]{0:T(1024)S(1)} %copy-done.74, bf16[960,80]{1,0:T(8,128)(2,1)S(1)} %copy-done.49, bf16[960,80]{1,0:T(8,128)(2,1)} %copy-done.50, bf16[960,80]{1,0:T(8,128)(2,1)} %copy-done.51, ...), kind=kOutput, calls=%fused_computation.103 | convolution fusion | flops 640776256 | bytes 15701632 | tf_op jit(solution)/shard_map/dot_general | solution.py:26
  542.8 5.3 pad_maximum_fusion.1
  548.0 132.7 %grad_scatter.1 = (f32[128,640]{1,0:T(8,128)}, f32[120,640]{1,0:T(8,128)}, f32[120,640]{1,0:T(8,128)}, f32[320,240]{1,0:T(8,128)}) custom-call(bf16[2,2,4,2,128,640]{5,4,3,2,1,0:T(8,128)(2,1)} %bitcast.496, bf16[2,2,4,2,120,640]{5,4,3,2,1,0:T(8,128)(2,1)} %bitcast.497, bf16[2,2,4,2,120,640]{5,4,3,2,1,0:T(8,128)(2,1)} %bitcast.498, ...), custom_call_target="tpu_custom_call" | custom-call | tf_op jit(solution)/shard_map/grad_scatter/pallas_call | solution.py:421
  686.3 9.4 %copy_bitcast_fusion.2 = (bf16[8,128,960]{1,2,0:T(8,128)(2,1)}, bf16[8,128,960]{1,2,0:T(8,128)(2,1)}) fusion(bf16[120,8,8,128]{3,2,1,0:T(8,128)(2,1)} %fusion.80, f32[8,120,8,128]{3,2,1,0:T(8,128)} %convert_bitcast_fusion, f32[1024,960]{0,1:T(8,128)} %get-tuple-element.341, f32[1024]{0:T(1024)S(1)} %fusion.180, f32[960]{0:T(1024)S(1)} %copy-done.74, ...), kind=kLoop, calls=%fused_computation.132 | loop fusion | flops 13762560 | bytes 23617024
  (366 shorter events, 237.2 us)
Async XLA Ops:
  7.2 269.0 %copy-start = (bf16[8,128,960]{1,2,0:T(8,128)(2,1)S(1)}, bf16[8,128,960]{1,2,0:T(8,128)(2,1)}, u32[]{:S(2)}) copy-start(bf16[8,128,960]{1,2,0:T(8,128)(2,1)} %param.27) | copy-start | bytes 5898244
  7.2 181.7 %all-gather.3.cloned.1.call-start = ((), (), s32[]{:S(2)}) async-start(), calls=%async_computation.2 | async-start | bytes 3276800 | tf_op jit(solution)/shard_map/all_gather | solution.py:642
  143.3 27.2 %copy-start.73 = (f32[960]{0:T(1024)}, f32[960]{0:T(1024)S(1)}, u32[]{:S(2)}) copy-start(f32[960]{0:T(1024)S(1)} %reshape.456) | copy-start | bytes 11524
  151.9 51.6 %all-gather.5.cloned.1.call-start = ((), (), s32[]{:S(2)}) async-start(), calls=%async_computation.3 | async-start | bytes 3276800 | tf_op jit(solution)/shard_map/all_gather | solution.py:641
  154.5 20.4 %copy-start.65 = (f32[128,32]{0,1:T(8,128)}, f32[128,32]{0,1:T(8,128)S(1)}, u32[]{:S(2)}) copy-start(f32[128,32]{0,1:T(8,128)S(1)} %get-tuple-element.337) | copy-start | bytes 49156
  158.2 335.5 %reduce-scatter.3.cloned.1.call-start = ((), (), s32[]{:S(2)}) async-start(), calls=%async_computation.4 | async-start | bytes 6553600 | tf_op jit(solution)/shard_map/reduce_scatter | solution.py:681
  177.3 138.8 %copy-start.77 = (f32[960]{0:T(1024)}, f32[960]{0:T(1024)S(1)}, u32[]{:S(2)}) copy-start(f32[960]{0:T(1024)S(1)} %reshape.457) | copy-start | bytes 11524
  188.9 87.2 %copy-start.34 = (bf16[2560,240]{1,0:T(8,128)(2,1)}, bf16[2560,240]{1,0:T(8,128)(2,1)S(1)}, u32[]{:S(2)}) copy-start(bf16[2560,240]{1,0:T(8,128)(2,1)S(1)} %get-tuple-element.281) | copy-start | bytes 3686404
  254.1 62.0 %copy-start.1 = (f32[1024,960]{0,1:T(8,128)}, f32[1024,960]{0,1:T(8,128)S(1)}, u32[]{:S(2)}) copy-start(f32[1024,960]{0,1:T(8,128)S(1)} %get-tuple-element.339) | copy-start | bytes 11796484
  254.1 62.0 %copy-start.79 = (f32[1024]{0:T(1024)}, f32[1024]{0:T(1024)S(1)}, u32[]{:S(2)}) copy-start(f32[1024]{0:T(1024)S(1)} %fusion.181) | copy-start | bytes 12292
  254.6 12.8 %copy-start.21 = (bf16[1024,960]{0,1:T(8,128)(2,1)}, bf16[1024,960]{0,1:T(8,128)(2,1)S(1)}, u32[]{:S(2)}) copy-start(bf16[1024,960]{0,1:T(8,128)(2,1)S(1)} %multiply_convert_fusion.1) | copy-start | bytes 5898244
  258.7 8.7 %copy-start.36 = (bf16[960,640]{1,0:T(8,128)(2,1)S(1)}, bf16[960,640]{1,0:T(8,128)(2,1)}, u32[]{:S(2)}) copy-start(bf16[960,640]{1,0:T(8,128)(2,1)} %get-tuple-element.289) | copy-start | bytes 3686404
  258.7 8.7 %copy-start.38 = (bf16[960,640]{1,0:T(8,128)(2,1)S(1)}, bf16[960,640]{1,0:T(8,128)(2,1)}, u32[]{:S(2)}) copy-start(bf16[960,640]{1,0:T(8,128)(2,1)} %get-tuple-element.290) | copy-start | bytes 3686404
  258.7 8.7 %copy-start.40 = (bf16[960,640]{1,0:T(8,128)(2,1)S(1)}, bf16[960,640]{1,0:T(8,128)(2,1)}, u32[]{:S(2)}) copy-start(bf16[960,640]{1,0:T(8,128)(2,1)} %get-tuple-element.291) | copy-start | bytes 3686404
  258.7 8.7 %copy-start.42 = (bf16[960,640]{1,0:T(8,128)(2,1)S(1)}, bf16[960,640]{1,0:T(8,128)(2,1)}, u32[]{:S(2)}) copy-start(bf16[960,640]{1,0:T(8,128)(2,1)} %get-tuple-element.292) | copy-start | bytes 3686404
  296.1 10.4 %copy-start.37 = (bf16[960,640]{1,0:T(8,128)(2,1)S(1)}, bf16[960,640]{1,0:T(8,128)(2,1)}, u32[]{:S(2)}) copy-start(bf16[960,640]{1,0:T(8,128)(2,1)} %get-tuple-element.289) | copy-start | bytes 3686404
  296.1 10.4 %copy-start.39 = (bf16[960,640]{1,0:T(8,128)(2,1)S(1)}, bf16[960,640]{1,0:T(8,128)(2,1)}, u32[]{:S(2)}) copy-start(bf16[960,640]{1,0:T(8,128)(2,1)} %get-tuple-element.290) | copy-start | bytes 3686404
  296.1 10.4 %copy-start.41 = (bf16[960,640]{1,0:T(8,128)(2,1)S(1)}, bf16[960,640]{1,0:T(8,128)(2,1)}, u32[]{:S(2)}) copy-start(bf16[960,640]{1,0:T(8,128)(2,1)} %get-tuple-element.291) | copy-start | bytes 3686404
  296.1 10.4 %copy-start.43 = (bf16[960,640]{1,0:T(8,128)(2,1)S(1)}, bf16[960,640]{1,0:T(8,128)(2,1)}, u32[]{:S(2)}) copy-start(bf16[960,640]{1,0:T(8,128)(2,1)} %get-tuple-element.292) | copy-start | bytes 3686404
  410.3 105.5 %reduce-scatter.5.cloned.1.call-start = ((), (), s32[]{:S(2)}) async-start(), calls=%async_computation.5 | async-start | bytes 6553600 | tf_op jit(solution)/shard_map/reduce_scatter | solution.py:682
  424.3 9.1 %slice-start.4 = ((s8[5242880]{0:T(1024)(128)(4,1)}), s8[4194304]{0:T(1024)(128)(4,1)S(1)}, s32[]{:S(2)}) async-start(s8[5242880]{0:T(1024)(128)(4,1)} %bitcast.537), calls=%async_computation.10 | async-start | bytes 8388608
  447.1 9.2 %slice-start.8 = ((s8[5242880]{0:T(1024)(128)(4,1)}), s8[4194304]{0:T(1024)(128)(4,1)S(1)}, s32[]{:S(2)}) async-start(s8[5242880]{0:T(1024)(128)(4,1)} %bitcast.541), calls=%async_computation.14 | async-start | bytes 8388608
  496.8 19.0 %copy-start.49 = (bf16[960,80]{1,0:T(8,128)(2,1)S(1)}, bf16[960,80]{1,0:T(8,128)(2,1)}, u32[]{:S(2)}) copy-start(bf16[960,80]{1,0:T(8,128)(2,1)} %copy-done.48) | copy-start | bytes 460804
  496.8 19.0 %copy-start.74 = (f32[960]{0:T(1024)S(1)}, f32[960]{0:T(1024)}, u32[]{:S(2)}) copy-start(f32[960]{0:T(1024)} %copy-done.73) | copy-start | bytes 11524
  496.9 19.0 %copy-start.76 = (f32[1024]{0:T(1024)S(1)}, f32[1024]{0:T(1024)}, u32[]{:S(2)}) copy-start(f32[1024]{0:T(1024)} %copy-done.75) | copy-start | bytes 12292
  548.0 136.8 %copy-start.72 = (f32[8,128]{1,0:T(8,128)S(1)}, f32[8,128]{1,0:T(8,128)}, u32[]{:S(2)}) copy-start(f32[8,128]{1,0:T(8,128)} %copy-done.71) | copy-start | bytes 12292
  548.0 138.2 %copy-start.78 = (f32[960]{0:T(1024)S(1)}, f32[960]{0:T(1024)}, u32[]{:S(2)}) copy-start(f32[960]{0:T(1024)} %copy-done.77) | copy-start | bytes 11524
  548.0 138.2 %copy-start.80 = (f32[1024]{0:T(1024)S(1)}, f32[1024]{0:T(1024)}, u32[]{:S(2)}) copy-start(f32[1024]{0:T(1024)} %copy-done.79) | copy-start | bytes 12292
  548.0 138.2 %copy-start.82 = (f32[1024]{0:T(1024)S(1)}, f32[1024]{0:T(1024)}, u32[]{:S(2)}) copy-start(f32[1024]{0:T(1024)} %copy-done.81) | copy-start | bytes 12292
  686.2 9.4 %copy-start.69 = (f32[120,640]{1,0:T(8,128)S(1)}, f32[120,640]{1,0:T(8,128)}, u32[]{:S(2)}) copy-start(f32[120,640]{1,0:T(8,128)} %get-tuple-element.554) | copy-start | bytes 921604
  686.2 10.1 %copy-start.68 = (f32[120,640]{1,0:T(8,128)S(1)}, f32[120,640]{1,0:T(8,128)}, u32[]{:S(2)}) copy-start(f32[120,640]{1,0:T(8,128)} %get-tuple-element.555) | copy-start | bytes 921604
  686.3 10.9 %copy-start.67 = (f32[320,240]{1,0:T(8,128)S(1)}, f32[320,240]{1,0:T(8,128)}, u32[]{:S(2)}) copy-start(f32[320,240]{1,0:T(8,128)} %get-tuple-element.556) | copy-start | bytes 921604
  (66 other events, 202.3 us)
Sparse Core Ops, SparseCore 0:
  152.0 23.9 all-gather.2
  177.5 25.8 all-gather.4
  410.4 51.3 reduce-scatter.2
  464.4 51.3 reduce-scatter.4
